TPU v7x, 256 devices: a whole 4x4x8 slice. The times are simulated.
256 devices in a mesh: dom: 8 (over y, x_hi), ref: 32 (over x_lo, z, core).
Axes of the slice: x: 4 (x_hi: 2, x_lo: 2; x = x_hi * 2 + x_lo), y: 4, z: 8, core: 2. Of those that a mesh axis runs over, the one named last changes fastest.
Arguments:
- particles: bfloat16 [2048, 16384], P(('dom', 'ref')), may hold values from -6 to 6
- offsets: int32 [2048, 2], P(('dom', 'ref')), may hold values from -6 to 6
- groups: int32 [2048], P(('dom', 'ref')), may hold values from 0 to 31
- precision: float32 [2048], P(('dom', 'ref')), may hold values from 0.05 to 16
- references: bfloat16 [8192, 16384], P('ref'), may hold values from -0.1796875 to 0.1796875
- ctf: float32 [32, 16384], replicated, may hold values from 0.25 to 1.75
- regularizer: float32 [8192], P('ref'), may hold values from 0.05 to 0.5
Outputs:
- new_references: float32 [16384, 8192], P('dom', 'ref')
- log_evidence: float32 [2048], P(('dom', 'ref'))
All inputs are finite; a program needn't handle non-finite values.
Results may differ from a plain program's by a relative error of at most 0.023.
Values may be sent and summed in bfloat16 or wider, within the bound.
No kernel may reach another device: no remote copies, remote signals or barrier semaphores. Data moves between devices by JAX's collectives and lax.ppermute only.
A program may use at most 128 MiB of HBM per device.

v0:
```python
import jax
import jax.numpy as jnp
from jax import lax
from jax.sharding import PartitionSpec as P

IMG = 128


def shift_images(images, offsets, side):
    squares = images.reshape(images.shape[0], side, side)

    def single(image, offset):
        return jnp.roll(image, (offset[0], offset[1]), axis=(0, 1))

    return jax.vmap(single)(squares, offsets).reshape(images.shape[0], side * side)


def local(particles, offsets, groups, precision, references, ctf, regularizer):
    group_count = ctf.shape[0]
    local_hot = (groups[:, None] == jnp.arange(group_count, dtype=jnp.int32)[None, :]).astype(
        jnp.float32
    )
    local_ctf = jnp.dot(local_hot, ctf, precision=lax.Precision.HIGHEST)
    shifted = shift_images(particles, offsets, IMG)
    filtered = (local_ctf * shifted.astype(jnp.float32)).astype(jnp.bfloat16)
    block_rows, block_groups, block_prec = (
        lax.all_gather(filtered, "ref", axis=0, tiled=True),
        lax.all_gather(groups, "ref", axis=0, tiled=True),
        lax.all_gather(precision.astype(jnp.bfloat16), "ref", axis=0, tiled=True).astype(
            precision.dtype
        ),
    )
    ref_float = references.astype(jnp.float32)
    ctf_square = ctf * ctf
    quad = lax.dot_general(
        ctf_square, ref_float * ref_float, (((1,), (1,)), ((), ())), precision=lax.Precision.HIGHEST
    )
    block_hot = (block_groups[:, None] == jnp.arange(group_count, dtype=jnp.int32)[None, :]).astype(
        jnp.float32
    )
    penalty = jnp.dot(block_hot, quad, precision=lax.Precision.HIGHEST)
    inner = lax.dot_general(
        block_rows, references, (((1,), (1,)), ((), ())), preferred_element_type=jnp.float32
    )
    scores = block_prec[:, None] * (inner - 0.5 * penalty)
    highest = lax.pmax(jnp.max(scores, axis=1), "ref")
    summed = lax.psum(jnp.sum(jnp.exp(scores - highest[:, None]), axis=1), "ref")
    log_block = highest + jnp.log(summed)
    weights = jnp.exp(scores - log_block[:, None])
    rounded = weights.astype(jnp.bfloat16)
    group_local = lax.dot_general(
        block_hot, weights, (((0,), (0,)), ((), ())), precision=lax.Precision.HIGHEST
    )
    pixels = references.shape[1]
    share = pixels // lax.axis_size("dom")
    first_pixel = lax.axis_index("dom") * share
    numerator = lax.psum_scatter(
        lax.dot_general(
            block_rows, rounded, (((0,), (0,)), ((), ())), preferred_element_type=jnp.float32
        ).astype(jnp.bfloat16),
        "dom",
        scatter_dimension=0,
        tiled=True,
    ).astype(jnp.float32)
    group_weights = lax.psum(group_local.astype(jnp.bfloat16), "dom").astype(jnp.float32)
    ctf_share = lax.dynamic_slice_in_dim(ctf_square, first_pixel, share, 1)
    denominator = lax.dot_general(
        ctf_share, group_weights, (((0,), (0,)), ((), ())), precision=lax.Precision.HIGHEST
    )
    new_references = numerator / (denominator + regularizer[None, :])
    own_rows = particles.shape[0]
    log_evidence = lax.dynamic_slice_in_dim(
        log_block, lax.axis_index("ref") * own_rows, own_rows, 0
    )
    return (new_references, log_evidence)


def solution(mesh):
    return jax.shard_map(
        local,
        mesh=mesh,
        in_specs=(
            P(("dom", "ref"), None),
            P(("dom", "ref"), None),
            P(("dom", "ref")),
            P(("dom", "ref")),
            P("ref", None),
            P(),
            P("ref"),
        ),
        out_specs=(P("dom", "ref"), P(("dom", "ref"))),
        check_vma=False,
    )
```

profile of v0, /device:TPU:1, one launch (start us, length us, event | category | flops | bytes accessed | tf_op | source)
XLA Modules:
  0.0 358.4 jit_solution(16345024495138774256)
XLA Ops:
  7.2 0.0 copy-start.4
  7.2 0.0 copy-start
  7.2 0.0 copy-start.1
  7.2 0.0 copy-start.3
  7.2 0.0 all-gather.2.cloned.1.call-start
  7.3 0.8 or_bitcast_fusion
  8.1 1.1 pad_maximum_fusion
  9.2 1.3 gather_fusion
  10.6 0.6 copy.9
  11.2 1.3 gather_fusion.1
  12.5 0.2 copy.10
  12.8 0.0 copy-done
  12.8 2.2 fusion
  15.0 0.0 all-gather.2.cloned.1.call-update
  15.0 0.0 reduce-scatter.2.cloned.1.call-start
  15.0 0.0 copy-done.3
  15.1 0.0 copy-done.4
  15.1 0.6 dynamic-slice
  16.3 0.2 dynamic-update-slice
  16.6 58.0 %all-reduce.2 = bf16[256]{0:T(256)(128)(2,1)S(1)} all-reduce(bf16[256]{0:T(256)(128)(2,1)S(1)} %dynamic-update-slice), channel_id=1, replica_groups=mesh['dom'=8,'ref'=32] {'ref'}, use_global_device_ids=true, to_apply=%add.2 | all-reduce | flops 256 | bytes 1024
  74.6 0.0 copy-done.1
  74.6 0.2 dynamic-update-slice.1
  74.8 13.0 %all-reduce.3 = s32[256]{0:T(256)S(1)} all-reduce(s32[256]{0:T(256)S(1)} %dynamic-update-slice.1), channel_id=1, replica_groups=mesh['dom'=8,'ref'=32] {'ref'}, use_global_device_ids=true, to_apply=%add.3 | all-reduce | flops 256 | bytes 2048
  87.8 17.0 %fusion.1 = f32[32,256]{1,0:T(8,128)S(1)} fusion(bf16[256,16384]{1,0:T(8,128)(2,1)} %param.11, f32[32,16384]{1,0:T(8,128)S(1)} %copy-done), kind=kOutput, calls=%fused_computation.5 | convolution fusion | flops 1619525632 | bytes 10518528 | tf_op jit(solution)/shard_map/dot_general | solution.py:35
  104.7 0.0 all-gather.2.cloned.1.call-done
  104.8 8.1 %fusion.24 = f32[256,256]{0,1:T(8,128)S(1)} fusion(bf16[256,16384]{1,0:T(8,128)(2,1)} %all-gather.2.cloned.1.call-done, bf16[256,16384]{1,0:T(8,128)(2,1)} %param.11), kind=kOutput, calls=%fused_computation.47 | convolution fusion | flops 2147483648 | bytes 17039360 | tf_op jit(solution)/shard_map/dot_general | solution.py:42
  112.9 0.4 fusion.23
  113.3 56.2 %pmax.7 = f32[256]{0:T(256)S(1)} all-reduce(f32[256]{0:T(256)S(1)} %get-tuple-element.4), channel_id=1, replica_groups=mesh['dom'=8,'ref'=32] {'ref'}, use_global_device_ids=true, to_apply=%region_1.2 | all-reduce | flops 256 | bytes 2048 | tf_op jit(solution)/shard_map/pmax | solution.py:46
  169.5 0.1 exponential_reduce_fusion
  169.5 53.6 %psum.14 = f32[256]{0:T(256)S(1)} all-reduce(f32[256]{0:T(256)S(1)} %exponential_reduce_fusion), channel_id=1, replica_groups=mesh['dom'=8,'ref'=32] {'ref'}, use_global_device_ids=true, to_apply=%region_3.4 | all-reduce | flops 256 | bytes 2048 | tf_op jit(solution)/shard_map/psum | solution.py:47
  223.1 9.0 %convolution_convert_fusion = bf16[16384,256]{1,0:T(8,128)(2,1)} fusion(bf16[256,16384]{1,0:T(8,128)(2,1)} %all-gather.2.cloned.1.call-done, f32[256,256]{0,1:T(8,128)S(1)} %get-tuple-element.5, f32[256]{0:T(256)S(1)} %log_add_fusion), kind=kOutput, calls=%fused_computation.2 | convolution fusion | flops 2151809024 | bytes 17040384 | tf_op jit(solution)/shard_map/dot_general | solution.py:58
  232.1 0.0 copy-start.2
  232.1 0.0 reduce-scatter.2.cloned.1.call-update
  232.2 1.6 mul.31
  233.8 0.6 dynamic_slice.7
  234.3 0.3 convolution_convert_fusion.1
  234.7 35.7 %psum.15 = bf16[32,256]{1,0:T(8,128)(2,1)S(1)} all-reduce(bf16[32,256]{1,0:T(8,128)(2,1)S(1)} %convolution_convert_fusion.1), channel_id=1, replica_groups=mesh['dom'=8,'ref'=32] {'dom'}, use_global_device_ids=true, to_apply=%region_5.6 | all-reduce | flops 8192 | bytes 32768 | tf_op jit(solution)/shard_map/psum | solution.py:65
  270.3 77.5 %reduce-scatter.2.cloned.1.call-done = bf16[2048,256]{1,0:T(8,128)(2,1)} async-done(((bf16[16384,256]{1,0:T(8,128)(2,1)}), bf16[2048,256]{1,0:T(8,128)(2,1)}) %reduce-scatter.2.cloned.1.call-update) | async-done | bytes 1048592 | tf_op jit(solution)/shard_map/reduce_scatter | solution.py:57
  347.8 0.0 copy-done.2
  347.8 3.7 %fusion.4 = f32[2048,256]{1,0:T(8,128)} fusion(bf16[32,256]{1,0:T(8,128)(2,1)S(1)} %psum.15, bf16[2048,256]{1,0:T(8,128)(2,1)} %reduce-scatter.2.cloned.1.call-done, f32[256]{0:T(256)S(1)} %copy-done.2, f32[32,16384]{1,0:T(8,128)} %mul.31, s32[]{:T(128)S(6)} %select_n.37), kind=kOutput, calls=%fused_computation.9 | convolution fusion | flops 202899456 | bytes 3425284 | tf_op jit(solution)/shard_map/dot_general | solution.py:67
  (6 shorter events, 0.1 us)
Async XLA Ops:
  7.2 7.9 %copy-start.4 = (u32[256]{0:T(256)S(1)}, u32[256]{0:T(256)}, u32[]{:S(2)}) copy-start(u32[256]{0:T(256)} %constant.114) | copy-start | bytes 3076
  7.2 5.6 %copy-start = (f32[32,16384]{1,0:T(8,128)S(1)}, f32[32,16384]{1,0:T(8,128)}, u32[]{:S(2)}) copy-start(f32[32,16384]{1,0:T(8,128)} %param.12) | copy-start | bytes 6291460
  7.2 67.4 %copy-start.1 = (s32[8]{0:T(128)S(1)}, s32[8]{0:T(128)}, u32[]{:S(2)}) copy-start(s32[8]{0:T(128)} %param.9) | copy-start | bytes 100
  7.2 7.8 %copy-start.3 = (f32[8]{0:T(128)S(1)}, f32[8]{0:T(128)}, u32[]{:S(2)}) copy-start(f32[8]{0:T(128)} %param.10) | copy-start | bytes 100
  7.2 97.5 %all-gather.2.cloned.1.call-start = ((), (), s32[]{:S(2)}) async-start(), calls=%async_computation.1 | async-start | bytes 8650752 | tf_op jit(solution)/shard_map/all_gather | solution.py:27
  15.0 332.8 %reduce-scatter.2.cloned.1.call-start = ((), (), s32[]{:S(2)}) async-start(), calls=%async_computation.2 | async-start | bytes 9437184 | tf_op jit(solution)/shard_map/reduce_scatter | solution.py:57
  232.1 115.7 %copy-start.2 = (f32[256]{0:T(256)S(1)}, f32[256]{0:T(256)}, u32[]{:S(2)}) copy-start(f32[256]{0:T(256)} %param.13) | copy-start | bytes 3076
Sparse Core Ops, SparseCore 0:
  15.1 76.8 all-gather.1
  232.3 115.4 reduce-scatter.1
where the time goes:
time: 359 us; the launch traced here: 358 us
  blocking collectives  216 us (60%)
  waiting for transfers between devices  77.5 us (22%)
  matrix products  40.7 us (11%)
  between operations  14.9 us (4%)
  local copies, waits for them, and re-layouts  5.16 us (1%)
  other arithmetic  3.69 us (1%)
    reduce_scatter x1, waiting for transfers between devices, local(): lax.psum_scatter(lax.dot_general(block_rows, rounded, (((0,), (0,)), ((),...  77.5 us
    unnamed x2, blocking collectives  70.9 us
    pmax x1, blocking collectives, local(): highest = lax.pmax(jnp.max(scores, axis=1), 'ref')  56.2 us
    psum x1, blocking collectives, local(): lax.psum(jnp.sum(jnp.exp(scores - highest[:, None]), axis=1), 'ref')  53.6 us
    psum x1, blocking collectives, local(): lax.psum(group_local.astype(jnp.bfloat16), 'dom').astype(jnp.float32)  35.7 us
    dot_general x1, matrix products, local(): lax.dot_general(ctf_square, ref_float * ref_float, (((1,), (1,)), ((), ()...  17 us
    dot_general x1, matrix products, local(): lax.dot_general(block_rows, rounded, (((0,), (0,)), ((), ())), preferred_...  9.03 us
    dot_general x1, matrix products, local(): lax.dot_general(block_rows, references, (((1,), (1,)), ((), ())), preferr...  8.13 us
  transfers between devices with their start and end apart: 2, of which 1 were waited for; matrix products, arithmetic and copies ran while one was open for 6% of the time, Pallas kernels for 0%

commit v1 on v0

v1 whole, which is shorter than its diff:
```python
import functools

import jax
import jax.numpy as jnp
import numpy as np
from jax import lax
from jax.experimental import pallas as pl
from jax.experimental.pallas import tpu as pltpu
from jax.sharding import PartitionSpec as P

IMG = 128
EXTRA = 128


VMEM = pl.BlockSpec(memory_space=pltpu.VMEM)
SMEM = pl.BlockSpec(memory_space=pltpu.SMEM)
ANY = pl.BlockSpec(memory_space=pl.ANY)
ROOM = pltpu.CompilerParams(vmem_limit_bytes=24 << 20)
WIDE = pltpu.CompilerParams(vmem_limit_bytes=56 << 20)


def rounded(value):
    return value.astype(jnp.bfloat16).astype(jnp.float32)


def split3(value):
    high = rounded(value)
    rest = value - high
    mid = rounded(rest)
    return high, mid, rest - mid


def filter_kernel(offsets, groups, precision, particles, ctf, out, planes, images, rows, sems):
    count, side = images.shape[0], IMG
    shares, _, width = out.shape
    pixels = width - EXTRA
    per_share = pixels // side
    whole = pltpu.make_async_copy(particles, images, sems.at[count])
    whole.start()
    copies = []
    for n in range(count):
        copy = pltpu.make_async_copy(ctf.at[pl.ds(groups[n], 1)], rows.at[pl.ds(n, 1)], sems.at[n])
        copy.start()
        copies.append(copy)
    lane = lax.broadcasted_iota(jnp.int32, (1, EXTRA), 1)
    slot = lax.broadcasted_iota(jnp.int32, (count, EXTRA), 0)
    extra = jnp.zeros((count, EXTRA), jnp.float32)
    for n in range(count):
        hot = jnp.where((lane < 96) & (lax.rem(lane, 32) == groups[n]), 1.0, 0.0)
        for part, value in enumerate(split3(jnp.full((1, EXTRA), precision[n], jnp.float32))):
            hot = jnp.where(lane == 96 + part, value, hot)
        extra = jnp.where(slot == n, hot, extra)
    extra = extra.astype(jnp.bfloat16)
    whole.wait()
    for line in range(side):
        planes[pl.ds(line, count, stride=side), :] = images[
            :, line * side : (line + 1) * side
        ].astype(jnp.float32)
    for n in range(count):
        image = planes[n * side : (n + 1) * side, :]
        image = pltpu.roll(image, lax.rem(offsets[0, n] + side, side), 0)
        image = pltpu.roll(image, lax.rem(offsets[1, n] + side, side), 1)
        planes[n * side : (n + 1) * side, :] = image
    for copy in copies:
        copy.wait()
    for share in range(shares):
        for line in range(per_share):
            at = share * per_share + line
            value = planes[pl.ds(at, count, stride=side), :] * rows[:, at * side : (at + 1) * side]
            out[share, :, line * side : (line + 1) * side] = value.astype(jnp.bfloat16)
        out[share, :, pixels:] = extra


def filtered_shares(particles, offsets, groups, precision, ctf, shares):
    images, pixels = particles.shape
    return pl.pallas_call(
        filter_kernel,
        out_shape=jax.ShapeDtypeStruct((shares, images, pixels // shares + EXTRA), jnp.bfloat16),
        in_specs=[SMEM, SMEM, SMEM, ANY, ANY],
        out_specs=VMEM,
        scratch_shapes=[
            pltpu.VMEM((images * IMG, IMG), jnp.float32),
            pltpu.VMEM((images, pixels), jnp.bfloat16),
            pltpu.VMEM((images, pixels), jnp.float32),
            pltpu.SemaphoreType.DMA((images + 1,)),
        ],
        compiler_params=WIDE,
    )(offsets.T, groups, precision, particles, ctf)


def table_kernel(place, references, ctf, table, part, filters, sems):
    share = part.shape[1]
    group = ctf.shape[0]
    first = pl.multiple_of(place[2] * share, share)
    one = pltpu.make_async_copy(ctf.at[:, pl.ds(first, share)], filters, sems.at[0])
    two = pltpu.make_async_copy(references.at[:, pl.ds(first, share)], part, sems.at[1])
    one.start()
    two.start()
    one.wait()
    two.wait()
    step = 256
    total = jnp.zeros((part.shape[0], EXTRA), jnp.float32)
    for at in range(0, share, step):
        value = part[:, at : at + step]
        table[:, at : at + step] = value
        value = value.astype(jnp.float32)
        value = value * value
        high = rounded(value)
        square = filters[:, at : at + step]
        square = jnp.concatenate(
            list(split3(square * square)) + [jnp.zeros((EXTRA - 3 * group, step), jnp.float32)], axis=0
        ).astype(jnp.bfloat16)
        for some in (high, value - high):
            total = total + lax.dot_general(
                some.astype(jnp.bfloat16), square, (((1,), (1,)), ((), ())), preferred_element_type=jnp.float32
            )
    quad = total + pltpu.roll(total, EXTRA - group, 1) + pltpu.roll(total, EXTRA - 2 * group, 1)
    lane = lax.broadcasted_iota(jnp.int32, quad.shape, 1)
    high, mid, low = split3(jnp.where(lane < group, -0.5 * quad, 0.0))
    table[:, share:] = (high + pltpu.roll(mid, group, 1) + pltpu.roll(low, 2 * group, 1)).astype(jnp.bfloat16)


def share_table(place, references, ctf, shares):
    rows, share = references.shape[0], references.shape[1] // shares
    return pl.pallas_call(
        table_kernel,
        out_shape=jax.ShapeDtypeStruct((rows, share + EXTRA), jnp.bfloat16),
        in_specs=[SMEM, ANY, ANY],
        out_specs=VMEM,
        scratch_shapes=[
            pltpu.VMEM((rows, share), jnp.bfloat16),
            pltpu.VMEM((ctf.shape[0], share), jnp.float32),
            pltpu.SemaphoreType.DMA((2,)),
        ],
        compiler_params=WIDE,
        cost_estimate=pl.CostEstimate(flops=1 << 29, bytes_accessed=8 << 20, transcendentals=0),
    )(place, references, ctf)


def score_kernel(counts, *refs):
    count = sum(counts)
    blocks, tables = refs[:count], refs[count : count + 4]
    out, lines = refs[count + 4 :]
    n_dom, rows, width = out.shape[0], out.shape[1], out.shape[2] // 4
    own = rows // len(counts)
    at = 0
    for block in blocks:
        lines[at : at + block.shape[0], :] = block[...]
        at += block.shape[0]
    share = lines.shape[1] - EXTRA
    extra = lines[:, share:].astype(jnp.float32)
    noise = extra[:, 96:97] + extra[:, 97:98] + extra[:, 98:99]
    for q, table in enumerate(tables):
        part = lax.dot_general(
            lines[...], table[...], (((1,), (1,)), ((), ())), preferred_element_type=jnp.float32
        )
        part = part * noise
        for o in range(len(counts)):
            for d in range(n_dom):
                at = (o * n_dom + d) * own
                out[d, o * own : (o + 1) * own, q * width : (q + 1) * width] = part[at : at + own, :]


def places_of(z_at, rows, own):
    line = lax.broadcasted_iota(jnp.int32, (rows, 2 * rows), 0)
    lane = lax.broadcasted_iota(jnp.int32, (rows, 2 * rows), 1)
    return lane, lax.rem(line + z_at * own, rows)


def soften_kernel(place, parts, score, stats):
    value = parts[0]
    for d in range(1, parts.shape[0]):
        value = value + parts[d]
    score[...] = value
    rows = value.shape[0]
    top = jnp.max(value, axis=1, keepdims=True)
    total = jnp.sum(jnp.exp(value - top), axis=1, keepdims=True)
    lane, target = places_of(place[1], rows, rows // stats.shape[0])
    both = jnp.where(lane == target, top, 0.0) + jnp.where(lane == target + rows, total, 0.0)
    stats[...] = jnp.broadcast_to(jnp.sum(both, axis=0, keepdims=True)[None], stats.shape)


def weigh_kernel(place, score, stats, spread, evidence, table):
    x_c, z_at = place[0], place[1]
    rows = score.shape[0]
    own = rows // stats.shape[0]
    tops = stats[...]
    sums = pltpu.roll(tops, rows, 1)
    highest = jnp.max(tops, axis=0, keepdims=True)
    total = jnp.sum(sums * jnp.exp(tops - highest), axis=0, keepdims=True)
    logged = highest + jnp.log(total)
    evidence[...] = logged
    lane, target = places_of(z_at, rows, own)
    column = jnp.sum(jnp.where(lane == target, logged, 0.0), axis=1, keepdims=True)
    value = jnp.exp(score[...] - column)
    for o in range(rows // own):
        at = pl.multiple_of(lax.rem(z_at + o, rows // own) * own, own)
        table[pl.ds(at, own), :] = value[o * own : (o + 1) * own, :]
    width = table.shape[1] // 4
    for q in range(4):
        part = table[:, q * width : (q + 1) * width].astype(jnp.bfloat16)
        for d in range(spread.shape[0] // 4):
            spread[d * 4 + (q ^ x_c)] = part


def divide_kernel(sums, square, regularizer, out):
    share, width = out.shape
    n_group = square.shape[1] // 4
    high = sums[share : share + n_group, :]
    first = high.astype(jnp.bfloat16).astype(jnp.float32)
    second = (high - first).astype(jnp.bfloat16)
    first = first.astype(jnp.bfloat16)
    factors = jnp.concatenate([first, first, second, jnp.zeros_like(second)], axis=0)
    step = 256
    for at in range(0, share, step):
        bottom = jnp.dot(square[at : at + step, :], factors, preferred_element_type=jnp.float32)
        out[at : at + step, :] = sums[at : at + step, :] / (bottom + regularizer[...])


def ring_tables(mesh):
    n_ref, n_dom = mesh.shape["ref"], mesh.shape["dom"]
    depth = n_ref // 4

    def along(step):
        return [(i, (i // (2 * depth)) * 2 * depth + (i + 2 * step) % (2 * depth)) for i in range(n_ref)]

    return {
        "core": ("ref", [(i, i ^ 1) for i in range(n_ref)]),
        "side": ("ref", [(i, (i + 2 * depth) % n_ref) for i in range(n_ref)]),
        "up": ("ref", along(1)),
        "down": ("ref", along(-1)),
        "column": [
            [x * 2 * depth + z * 2 + c for z in range(depth)] for x in range(2) for c in range(2)
        ],
        "same_z": [
            [d * n_ref + x * 2 * depth + z * 2 + c for d in range(n_dom) for x in range(2) for c in range(2)]
            for z in range(depth)
        ],
    }


def local(tables, particles, offsets, groups, precision, references, ctf, regularizer):
    def send(name, value):
        axis, pairs = tables[name]
        return lax.ppermute(value, axis, pairs)

    dom = lax.axis_index("dom")
    ref = lax.axis_index("ref")
    n_dom = lax.axis_size("dom")
    n_ref = lax.axis_size("ref")
    depth = n_ref // 4
    x_at, z_at, c_at = ref // (2 * depth), (ref // 2) % depth, ref % 2
    own, pixels = particles.shape
    share = pixels // n_dom
    n_group = ctf.shape[0]
    n_own_ref = references.shape[0]

    pieces = filtered_shares(particles, offsets, groups, precision, ctf, n_dom)

    place = jnp.stack([x_at * 2 + c_at, z_at, dom])
    table = share_table(lax.optimization_barrier((place, pieces))[0], references, ctf, n_dom)
    ctf_share = lax.dynamic_slice_in_dim(ctf, dom * share, share, 1)
    square_t = (ctf_share * ctf_share).T
    square_high = lax.reduce_precision(square_t, 8, 7)
    square = jnp.concatenate(
        [square_high, square_t - square_high, square_high, jnp.zeros_like(square_t)], axis=1
    ).astype(jnp.bfloat16)
    block = lax.all_to_all(pieces, "dom", 0, 0, tiled=True)
    block = block.reshape(n_dom * own, share + EXTRA)
    half = block.shape[0] // 2
    table_x = send("side", table)
    beside = send("side", block)

    held = {0: [block]}
    up = down = block
    for step in range(1, depth // 2):
        up, down = send("up", up), send("down", down)
        held[depth - step] = [up]
        held[step] = [down]
    table_x = lax.optimization_barrier((table_x, up, down))[0]
    beside = lax.optimization_barrier((beside, up, down))[0]
    held[depth // 2] = [send("up", up[:half]), send("down", down[half:])]
    beside = lax.all_gather(beside, "ref", axis=0, tiled=True, axis_index_groups=tables["column"])
    tables4 = [table, send("core", table), table_x, send("core", table_x)]

    rows = depth * own
    blocks = [held[o] for o in range(depth)]
    counts = [len(v) for v in blocks]
    parts, mine = pl.pallas_call(
        functools.partial(score_kernel, counts),
        out_shape=(
            jax.ShapeDtypeStruct((n_dom, rows, 4 * n_own_ref), jnp.float32),
            jax.ShapeDtypeStruct((n_dom * rows, share + EXTRA), jnp.bfloat16),
        ),
        in_specs=[VMEM] * (sum(counts) + 4),
        out_specs=(VMEM, VMEM),
        compiler_params=ROOM,
    )(*[v for some in blocks for v in some], *tables4)
    parts = lax.all_to_all(parts, "dom", 0, 0, tiled=True)

    score, stats = pl.pallas_call(
        soften_kernel,
        out_shape=(
            jax.ShapeDtypeStruct((rows, 4 * n_own_ref), jnp.float32),
            jax.ShapeDtypeStruct((depth, 1, 2 * rows), jnp.float32),
        ),
        in_specs=[SMEM, VMEM],
        out_specs=(VMEM, VMEM),
        compiler_params=ROOM,
    )(place, parts)
    stats = lax.all_to_all(stats, "ref", 0, 0, tiled=True, axis_index_groups=tables["column"])
    weights, evidence = pl.pallas_call(
        weigh_kernel,
        out_shape=(
            jax.ShapeDtypeStruct((4 * n_dom, rows, n_own_ref), jnp.bfloat16),
            jax.ShapeDtypeStruct((1, 2 * rows), jnp.float32),
        ),
        in_specs=[SMEM, VMEM, VMEM],
        out_specs=(VMEM, VMEM),
        scratch_shapes=[pltpu.VMEM((rows, 4 * n_own_ref), jnp.float32)],
        compiler_params=ROOM,
    )(place, score, stats.reshape(depth, 2 * rows))
    log_evidence = lax.dynamic_slice(evidence, (0, z_at * own), (1, own)).reshape(own)
    weights = lax.all_to_all(
        weights, ("dom", "ref"), 0, 0, tiled=True, axis_index_groups=tables["same_z"]
    )
    weights = weights.reshape(n_dom, 2, 2, depth, own, n_own_ref)

    def order(x, c, turn):
        some = lax.dynamic_slice(
            weights, (0, x, c, 0, 0, 0), (n_dom, 1, 1, depth, own, n_own_ref)
        ).reshape(n_dom, depth, own, n_own_ref)
        if turn:
            some = lax.dynamic_slice_in_dim(jnp.concatenate([some, some], axis=1), z_at, depth, 1)
        return some.transpose(1, 0, 2, 3).reshape(-1, n_own_ref)

    sums = 0.0
    for some, side in ((mine, 0), (beside, 1)):
        for rows_of, core in ((some, 0), (send("core", some), 1)):
            weight = order((x_at + side) % 2, (c_at + core) % 2, side == 0)
            sums = sums + lax.dot_general(
                rows_of, weight, (((0,), (0,)), ((), ())), preferred_element_type=jnp.float32
            )
    new_references = pl.pallas_call(
        divide_kernel,
        out_shape=jax.ShapeDtypeStruct((share, n_own_ref), jnp.float32),
        in_specs=[VMEM, VMEM, VMEM],
        out_specs=VMEM,
        compiler_params=ROOM,
    )(sums, square, regularizer[None, :])
    return new_references, log_evidence


def solution(mesh):
    return jax.shard_map(
        functools.partial(local, ring_tables(mesh)),
        mesh=mesh,
        in_specs=(
            P(("dom", "ref"), None),
            P(("dom", "ref"), None),
            P(("dom", "ref")),
            P(("dom", "ref")),
            P("ref", None),
            P(),
            P("ref"),
        ),
        out_specs=(P("dom", "ref"), P(("dom", "ref"))),
        check_vma=False,
    )
```

time: 359 us -> 163 us (0.45)
  blocking collectives: 216 us -> 0 us
  starting transfers between devices: 0.08 us -> 49.5 us
  matrix products: 40.7 us -> 4.96 us
  Pallas kernels: 0 us -> 14.7 us
  waiting for transfers between devices: 77.5 us -> 66.7 us
    psum x2 -> x0, blocking collectives: 89.2 us -> none  [the longest x1 53.6 us: local(): lax.psum(jnp.sum(jnp.exp(scores - highest[:, None]), axis=1), 'ref')]
    reduce_scatter x1 -> x0, waiting for transfers between devices: 77.5 us -> none  [local(): lax.psum_scatter(lax.dot_general(block_rows, rounded, (((0,), (0,)), ((),...]
    unnamed x2 -> x0, blocking collectives: 70.9 us -> none
    pmax x1 -> x0, blocking collectives: 56.2 us -> none  [local(): highest = lax.pmax(jnp.max(scores, axis=1), 'ref')]
    all_to_all x0 -> x4, waiting for transfers between devices: none -> 47.3 us  [the longest x1 26.1 us: local(): parts = lax.all_to_all(parts, 'dom', 0, 0, tiled=True)]
    dot_general x7 -> x4, matrix products: 40.7 us -> 4.96 us  [local(): lax.dot_general(rows_of, weight, (((0,), (0,)), ((), ())), preferred_elem...]
    all_to_all x0 -> x4, starting transfers between devices: none -> 27.2 us  [the longest x1 8.21 us: local(): lax.all_to_all(weights, ('dom', 'ref'), 0, 0, tiled=True, axis_index_grou...]
    ppermute x0 -> x14, starting transfers between devices: none -> 22.2 us  [send(): return lax.ppermute(value, axis, pairs)]
  transfers between devices with their start and end apart: 2 -> 19, of which waited for: 1 -> 8; matrix products, arithmetic and copies ran while one was open for 6% -> 7% of each run, Pallas kernels for 0% -> 6%
where the time goes in v1:
time: 163 us; the launch traced here: 162 us
  waiting for transfers between devices  66.7 us (41%)
  starting transfers between devices  49.5 us (30%)
  Pallas kernels  14.7 us (9%)
  between operations  14.4 us (9%)
  local copies, waits for them, and re-layouts  8.35 us (5%)
  matrix products  4.96 us (3%)
  other arithmetic  3.7 us (2%)
    all_to_all x1, waiting for transfers between devices, local(): parts = lax.all_to_all(parts, 'dom', 0, 0, tiled=True)  26.1 us
    ppermute x14, starting transfers between devices, send(): return lax.ppermute(value, axis, pairs)  22.2 us
    ppermute x14, waiting for transfers between devices, send(): return lax.ppermute(value, axis, pairs)  19.4 us
    all_to_all x1, waiting for transfers between devices, local(): lax.all_to_all(weights, ('dom', 'ref'), 0, 0, tiled=True, axis_index_grou...  13.5 us
    all_to_all x1, starting transfers between devices, local(): lax.all_to_all(weights, ('dom', 'ref'), 0, 0, tiled=True, axis_index_grou...  8.21 us
    all_to_all x1, starting transfers between devices, local(): block = lax.all_to_all(pieces, 'dom', 0, 0, tiled=True)  7.49 us
    all_to_all x1, starting transfers between devices, local(): parts = lax.all_to_all(parts, 'dom', 0, 0, tiled=True)  6.87 us
    unnamed x17, local copies, waits for them, and re-layouts  5.19 us
  transfers between devices with their start and end apart: 19, of which 8 were waited for; matrix products, arithmetic and copies ran while one was open for 7% of the time, Pallas kernels for 6%

profile of v1, /device:TPU:1, one launch (start us, length us, event | category | flops | bytes accessed | tf_op | source)
XLA Modules:
  0.0 162.3 jit_solution(17473563323994843561)
XLA Ops:
  7.2 3.3 %shard_map.86 = bf16[8,8,2176]{2,1,0:T(8,128)(2,1)} custom-call(s32[2,8]{1,0:T(2,128)} %bitcast.51, s32[8]{0:T(128)} %groups.1, f32[8]{0:T(128)} %precision.1, bf16[8,16384]{1,0:T(8,128)(2,1)} %particles.1, f32[32,16384]{1,0:T(8,128)} %ctf.3), custom_call_target="tpu_custom_call" | custom-call | tf_op jit(solution)/shard_map/pallas_call | solution.py:76
  10.4 7.5 %all-to-all-start = ((bf16[8,8,2176]{2,1,0:T(8,128)(2,1)}), bf16[8,8,2176]{2,1,0:T(8,128)(2,1)S(1)}, u32[]{:S(2)}, u32[]{:S(2)}) async-start(bf16[8,8,2176]{2,1,0:T(8,128)(2,1)} %shard_map.86), calls=%async_computation | async-start | bytes 557056 | tf_op jit(solution)/shard_map/all_to_all | solution.py:268
  17.9 0.0 all-gather.2.cloned.1.call-start
  18.0 0.7 pad_add_fusion.place
  18.7 3.9 %shard_map.87.refs_9_ = bf16[256,2176]{1,0:T(8,128)(2,1)} custom-call(s32[3]{0:T(128)} %pad_add_fusion.place, bf16[256,16384]{1,0:T(8,128)(2,1)} %references.1, f32[32,16384]{1,0:T(8,128)} %ctf.3), custom_call_target="tpu_custom_call" | custom-call | flops 536870912 | bytes 8388608 | tf_op jit(solution)/shard_map/pallas_call | solution.py:125
  22.5 0.4 collective-permute-start.9
  22.9 2.7 %all-to-all-done = bf16[8,8,2176]{2,1,0:T(8,128)(2,1)S(1)} async-done(((bf16[8,8,2176]{2,1,0:T(8,128)(2,1)}), bf16[8,8,2176]{2,1,0:T(8,128)(2,1)S(1)}, u32[]{:S(2)}, u32[]{:S(2)}) %all-to-all-start) | async-done | bytes 278560 | tf_op jit(solution)/shard_map/all_to_all | solution.py:268
  25.7 5.6 %collective-permute-start = (bf16[64,2176]{1,0:T(8,128)(2,1)S(1)}, bf16[64,2176]{1,0:T(8,128)(2,1)S(1)}, u32[]{:S(2)}, u32[]{:S(2)}) collective-permute-start(bf16[64,2176]{1,0:T(8,128)(2,1)S(1)} %bitcast.41), channel_id=1, source_target_pairs={{0,14},{1,15},{2,0},{3,1},{4,2},{5,3},{6,4},{7,5},{8,6},{9,7},{10,... | collective-permute-start | bytes 835592 | tf_op jit(solution)/shard_map/ppermute | solution.py:245
  31.2 0.0 collective-permute-start.3
  31.2 3.8 %collective-permute-done.refs_1_ = bf16[64,2176]{1,0:T(8,128)(2,1)S(1)} collective-permute-done((bf16[64,2176]{1,0:T(8,128)(2,1)S(1)}, bf16[64,2176]{1,0:T(8,128)(2,1)S(1)}, u32[]{:S(2)}, u32[]{:S(2)}) %collective-permute-start) | collective-permute-done | bytes 278560 | tf_op jit(solution)/shard_map/ppermute | solution.py:245
  35.0 3.4 %collective-permute-start.1 = (bf16[64,2176]{1,0:T(8,128)(2,1)S(1)}, bf16[64,2176]{1,0:T(8,128)(2,1)S(1)}, u32[]{:S(2)}, u32[]{:S(2)}) collective-permute-start(bf16[64,2176]{1,0:T(8,128)(2,1)S(1)} %collective-permute-done.refs_1_), channel_id=1, source_target_pairs={{0,14},{1,15},{2,0},{3,1},{4,2},{5,3},{6,4},{7,5},{8,6},{9,7},{10,... | collective-permute-start | bytes 835592 | tf_op jit(solution)/shard_map/ppermute | solution.py:245
  38.4 0.0 collective-permute-done.3.refs_8_
  38.4 0.0 collective-permute-start.4
  38.4 0.3 collective-permute-start.12
  38.8 3.2 %collective-permute-done.1.refs_2_ = bf16[64,2176]{1,0:T(8,128)(2,1)S(1)} collective-permute-done((bf16[64,2176]{1,0:T(8,128)(2,1)S(1)}, bf16[64,2176]{1,0:T(8,128)(2,1)S(1)}, u32[]{:S(2)}, u32[]{:S(2)}) %collective-permute-start.1) | collective-permute-done | bytes 278560 | tf_op jit(solution)/shard_map/ppermute | solution.py:245
  41.9 3.1 %collective-permute-start.2 = (bf16[64,2176]{1,0:T(8,128)(2,1)S(1)}, bf16[64,2176]{1,0:T(8,128)(2,1)S(1)}, u32[]{:S(2)}, u32[]{:S(2)}) collective-permute-start(bf16[64,2176]{1,0:T(8,128)(2,1)S(1)} %collective-permute-done.1.refs_2_), channel_id=1, source_target_pairs={{0,14},{1,15},{2,0},{3,1},{4,2},{5,3},{6,4},{7,5},{8,6},{9,7},{10,... | collective-permute-start | bytes 835592 | tf_op jit(solution)/shard_map/ppermute | solution.py:245
  45.1 0.0 collective-permute-done.4.refs_7_
  45.1 0.0 collective-permute-start.5
  45.1 8.9 %collective-permute-done.12 = bf16[64,2176]{1,0:T(8,128)(2,1)S(1)} collective-permute-done((bf16[64,2176]{1,0:T(8,128)(2,1)S(1)}, bf16[64,2176]{1,0:T(8,128)(2,1)S(1)}, u32[]{:S(2)}, u32[]{:S(2)}) %collective-permute-start.12) | collective-permute-done | bytes 278560 | tf_op jit(solution)/shard_map/ppermute | solution.py:245
  53.9 0.0 collective-permute-done.2.refs_3_
  53.9 0.0 collective-permute-done.5.refs_6_
  53.9 0.7 copy-done.7
  54.7 0.0 all-gather.2.cloned.1.call-update
  54.7 2.9 %collective-permute-start.8 = (bf16[256,2176]{1,0:T(8,128)(2,1)}, bf16[256,2176]{1,0:T(8,128)(2,1)S(1)}, u32[]{:S(2)}, u32[]{:S(2)}) collective-permute-start(bf16[256,2176]{1,0:T(8,128)(2,1)} %shard_map.87.refs_9_), channel_id=1, source_target_pairs={{0,1},{1,0},{2,3},{3,2},{4,5},{5,4},{6,7},{7,6},{8,9},{9,8},{10,11... | collective-permute-start | bytes 3342344 | tf_op jit(solution)/shard_map/ppermute | solution.py:245
  57.6 0.0 collective-permute-done.9.refs_11_
  57.6 0.1 collective-permute-start.10
  57.7 0.8 collective-permute-start.6
  58.5 4.0 %collective-permute-start.7 = (bf16[32,2176]{1,0:T(8,128)(2,1)S(1)}, bf16[32,2176]{1,0:T(8,128)(2,1)S(1)}, u32[]{:S(2)}, u32[]{:S(2)}) collective-permute-start(bf16[32,2176]{1,0:T(8,128)(2,1)S(1)} %slice.9), channel_id=1, source_target_pairs={{0,14},{1,15},{2,0},{3,1},{4,2},{5,3},{6,4},{7,5},{8,6},{9,7},{10,... | collective-permute-start | bytes 417800 | tf_op jit(solution)/shard_map/ppermute | solution.py:245
  62.5 0.0 collective-permute-done.8.refs_10_
  62.5 3.6 %collective-permute-done.6.refs_4_ = bf16[32,2176]{1,0:T(8,128)(2,1)S(1)} collective-permute-done((bf16[32,2176]{1,0:T(8,128)(2,1)S(1)}, bf16[32,2176]{1,0:T(8,128)(2,1)S(1)}, u32[]{:S(2)}, u32[]{:S(2)}) %collective-permute-start.6) | collective-permute-done | bytes 139296 | tf_op jit(solution)/shard_map/ppermute | solution.py:245
  66.1 0.0 collective-permute-done.7.refs_5_
  66.1 0.0 collective-permute-done.10.refs_12_
  66.1 1.2 copy-done
  67.4 2.6 %shard_map.88 = (f32[8,64,1024]{2,1,0:T(8,128)S(1)}, bf16[512,2176]{1,0:T(8,128)(2,1)S(1)}) custom-call(bf16[64,2176]{1,0:T(8,128)(2,1)S(1)} %bitcast.44, bf16[64,2176]{1,0:T(8,128)(2,1)S(1)} %collective-permute-done.refs_1_, bf16[64,2176]{1,0:T(8,128)(2,1)S(1)} %collective-permute-done.1.refs_2_, bf16[64,2176]{1,0:T(8,128)(2,1)S(1)} %collective-permute-done.2.refs_3_, ...), custom_call_target="tpu_custom_call" | custom-call | tf_op jit(solution)/shard_map/pallas_call | solution.py:289
  70.0 1.4 copy-done.1
  71.4 1.3 copy-done.3
  72.8 6.9 %all-to-all-start.1 = ((f32[8,64,1024]{2,1,0:T(8,128)}), f32[8,64,1024]{2,1,0:T(8,128)S(1)}, u32[]{:S(2)}, u32[]{:S(2)}) async-start(f32[8,64,1024]{2,1,0:T(8,128)} %copy-done.3), calls=%async_computation.1 | async-start | bytes 4194304 | tf_op jit(solution)/shard_map/all_to_all | solution.py:299
  79.6 1.2 collective-permute-start.11
  80.8 26.1 %all-to-all-done.1.parts = f32[8,64,1024]{2,1,0:T(8,128)S(1)} async-done(((f32[8,64,1024]{2,1,0:T(8,128)}), f32[8,64,1024]{2,1,0:T(8,128)S(1)}, u32[]{:S(2)}, u32[]{:S(2)}) %all-to-all-start.1) | async-done | bytes 2097184 | tf_op jit(solution)/shard_map/all_to_all | solution.py:299
  106.9 1.4 shard_map.89
  108.3 4.7 %all-to-all-start.2 = ((f32[8,1,128]{2,1,0:T(1,128)}), f32[8,1,128]{2,1,0:T(1,128)S(1)}, u32[]{:S(2)}, u32[]{:S(2)}) async-start(f32[8,1,128]{2,1,0:T(1,128)} %get-tuple-element.16), calls=%async_computation.2 | async-start | bytes 8192 | tf_op jit(solution)/shard_map/all_to_all | solution.py:311
  113.0 1.0 constant_dynamic-slice_fusion.1
  114.0 0.3 copy.27
  114.4 0.1 pad.3.clone
  114.5 4.9 %all-to-all-done.2 = f32[8,1,128]{2,1,0:T(1,128)S(1)} async-done(((f32[8,1,128]{2,1,0:T(1,128)}), f32[8,1,128]{2,1,0:T(1,128)S(1)}, u32[]{:S(2)}, u32[]{:S(2)}) %all-to-all-start.2) | async-done | bytes 4128 | tf_op jit(solution)/shard_map/all_to_all | solution.py:311
  119.4 1.8 %shard_map.90 = (bf16[32,64,256]{2,1,0:T(8,128)(2,1)}, f32[1,128]{1,0:T(1,128)S(1)}) custom-call(s32[3]{0:T(128)S(1)} %copy-done.4, f32[64,1024]{1,0:T(8,128)S(1)} %get-tuple-element.15.score, f32[8,128]{1,0:T(8,128)S(1)} %bitcast.45), custom_call_target="tpu_custom_call" | custom-call | tf_op jit(solution)/shard_map/pallas_call | solution.py:312
  121.2 8.2 %all-to-all-start.3 = ((bf16[32,64,256]{2,1,0:T(8,128)(2,1)}), bf16[32,64,256]{2,1,0:T(8,128)(2,1)}, u32[]{:S(2)}, u32[]{:S(2)}) async-start(bf16[32,64,256]{2,1,0:T(8,128)(2,1)} %get-tuple-element.17), calls=%async_computation.3 | async-start | bytes 2097152 | tf_op jit(solution)/shard_map/all_to_all | solution.py:324
  129.4 1.0 fusion.1
  130.5 0.4 collective-permute-start.13
  130.9 1.8 %maximum_maximum_fusion.square = bf16[2048,128]{1,0:T(8,128)(2,1)S(1)} fusion(bf16[2048,32]{1,0:T(8,128)(2,1)} %get-tuple-element.21, bf16[2048,32]{1,0:T(8,128)(2,1)S(1)} %get-tuple-element.20, bf16[128]{0:T(256)(128)(2,1)S(1)} %pad.3.clone), kind=kLoop, calls=%fused_computation.10 | loop fusion | flops 2097152 | bytes 786688 | tf_op jit(solution)/shard_map/concatenate | solution.py:265
  132.6 0.6 fusion.4
  133.2 13.5 %all-to-all-done.3 = bf16[32,64,256]{2,1,0:T(8,128)(2,1)} async-done(((bf16[32,64,256]{2,1,0:T(8,128)(2,1)}), bf16[32,64,256]{2,1,0:T(8,128)(2,1)}, u32[]{:S(2)}, u32[]{:S(2)}) %all-to-all-start.3) | async-done | bytes 1048608 | tf_op jit(solution)/shard_map/all_to_all | solution.py:324
  146.8 1.4 constant_dynamic-slice_fusion.2
  148.3 0.1 fusion.3
  148.4 0.1 fusion.2
  148.5 0.2 copy-done.6
  148.7 0.8 fusion.6
  149.5 0.0 collective-permute-done.11
  149.5 2.6 %fusion.5 = f32[2176,256]{1,0:T(8,128)S(1)} fusion(bf16[512,2176]{1,0:T(8,128)(2,1)} %collective-permute-done.11, bf16[512,256]{1,0:T(8,128)(2,1)S(1)} %bitcast.47), kind=kOutput, calls=%fused_computation.23 | convolution fusion | flops 570425344 | bytes 4718592 | tf_op jit(solution)/shard_map/dot_general | solution.py:341
  152.1 0.8 fusion
  152.9 0.0 collective-permute-done.13
  152.9 0.0 copy-start.5
  152.9 0.8 convolution_add_fusion.sums
  153.7 1.7 %shard_map.91 = f32[2048,256]{1,0:T(8,128)} custom-call(f32[2176,256]{1,0:T(8,128)S(1)} %convolution_add_fusion.sums, bf16[2048,128]{1,0:T(8,128)(2,1)S(1)} %maximum_maximum_fusion.square, f32[1,256]{1,0:T(1,128)S(1)} %bitcast.46), custom_call_target="tpu_custom_call" | custom-call | tf_op jit(solution)/shard_map/pallas_call | solution.py:344
  (17 shorter events, 0.1 us)
Async XLA Ops:
  10.4 15.2 %all-to-all-start = ((bf16[8,8,2176]{2,1,0:T(8,128)(2,1)}), bf16[8,8,2176]{2,1,0:T(8,128)(2,1)S(1)}, u32[]{:S(2)}, u32[]{:S(2)}) async-start(bf16[8,8,2176]{2,1,0:T(8,128)(2,1)} %shard_map.86), calls=%async_computation | async-start | bytes 557056 | tf_op jit(solution)/shard_map/all_to_all | solution.py:268
  17.9 112.5 %all-gather.2.cloned.1.call-start = ((), (), s32[]{:S(2)}) async-start(), calls=%async_computation.4 | async-start | bytes 2506752 | tf_op jit(solution)/shard_map/all_gather | solution.py:283
  22.5 35.0 %collective-permute-start.9 = (bf16[256,2176]{1,0:T(8,128)(2,1)}, bf16[256,2176]{1,0:T(8,128)(2,1)S(1)}, u32[]{:S(2)}, u32[]{:S(2)}) collective-permute-start(bf16[256,2176]{1,0:T(8,128)(2,1)} %shard_map.87.refs_9_), channel_id=1, source_target_pairs={{0,16},{1,17},{2,18},{3,19},{4,20},{5,21},{6,22},{7,23},{8,24},{9,... | collective-permute-start | bytes 3342344 | tf_op jit(solution)/shard_map/ppermute | solution.py:245
  25.7 9.4 %collective-permute-start = (bf16[64,2176]{1,0:T(8,128)(2,1)S(1)}, bf16[64,2176]{1,0:T(8,128)(2,1)S(1)}, u32[]{:S(2)}, u32[]{:S(2)}) collective-permute-start(bf16[64,2176]{1,0:T(8,128)(2,1)S(1)} %bitcast.41), channel_id=1, source_target_pairs={{0,14},{1,15},{2,0},{3,1},{4,2},{5,3},{6,4},{7,5},{8,6},{9,7},{10,... | collective-permute-start | bytes 835592 | tf_op jit(solution)/shard_map/ppermute | solution.py:245
  31.2 7.2 %collective-permute-start.3 = (bf16[64,2176]{1,0:T(8,128)(2,1)S(1)}, bf16[64,2176]{1,0:T(8,128)(2,1)S(1)}, u32[]{:S(2)}, u32[]{:S(2)}) collective-permute-start(bf16[64,2176]{1,0:T(8,128)(2,1)S(1)} %bitcast.42), channel_id=1, source_target_pairs={{0,2},{1,3},{2,4},{3,5},{4,6},{5,7},{6,8},{7,9},{8,10},{9,11},{10,... | collective-permute-start | bytes 835592 | tf_op jit(solution)/shard_map/ppermute | solution.py:245
  35.0 6.9 %collective-permute-start.1 = (bf16[64,2176]{1,0:T(8,128)(2,1)S(1)}, bf16[64,2176]{1,0:T(8,128)(2,1)S(1)}, u32[]{:S(2)}, u32[]{:S(2)}) collective-permute-start(bf16[64,2176]{1,0:T(8,128)(2,1)S(1)} %collective-permute-done.refs_1_), channel_id=1, source_target_pairs={{0,14},{1,15},{2,0},{3,1},{4,2},{5,3},{6,4},{7,5},{8,6},{9,7},{10,... | collective-permute-start | bytes 835592 | tf_op jit(solution)/shard_map/ppermute | solution.py:245
  38.4 6.6 %collective-permute-start.4 = (bf16[64,2176]{1,0:T(8,128)(2,1)S(1)}, bf16[64,2176]{1,0:T(8,128)(2,1)S(1)}, u32[]{:S(2)}, u32[]{:S(2)}) collective-permute-start(bf16[64,2176]{1,0:T(8,128)(2,1)S(1)} %collective-permute-done.3.refs_8_), channel_id=1, source_target_pairs={{0,2},{1,3},{2,4},{3,5},{4,6},{5,7},{6,8},{7,9},{8,10},{9,11},{10,... | collective-permute-start | bytes 835592 | tf_op jit(solution)/shard_map/ppermute | solution.py:245
  38.4 15.5 %collective-permute-start.12 = (bf16[64,2176]{1,0:T(8,128)(2,1)S(1)}, bf16[64,2176]{1,0:T(8,128)(2,1)S(1)}, u32[]{:S(2)}, u32[]{:S(2)}) collective-permute-start(bf16[64,2176]{1,0:T(8,128)(2,1)S(1)} %bitcast.43), channel_id=1, source_target_pairs={{0,16},{1,17},{2,18},{3,19},{4,20},{5,21},{6,22},{7,23},{8,24},{9,... | collective-permute-start | bytes 835592 | tf_op jit(solution)/shard_map/ppermute | solution.py:245
  41.9 12.0 %collective-permute-start.2 = (bf16[64,2176]{1,0:T(8,128)(2,1)S(1)}, bf16[64,2176]{1,0:T(8,128)(2,1)S(1)}, u32[]{:S(2)}, u32[]{:S(2)}) collective-permute-start(bf16[64,2176]{1,0:T(8,128)(2,1)S(1)} %collective-permute-done.1.refs_2_), channel_id=1, source_target_pairs={{0,14},{1,15},{2,0},{3,1},{4,2},{5,3},{6,4},{7,5},{8,6},{9,7},{10,... | collective-permute-start | bytes 835592 | tf_op jit(solution)/shard_map/ppermute | solution.py:245
  45.1 8.9 %collective-permute-start.5 = (bf16[64,2176]{1,0:T(8,128)(2,1)S(1)}, bf16[64,2176]{1,0:T(8,128)(2,1)S(1)}, u32[]{:S(2)}, u32[]{:S(2)}) collective-permute-start(bf16[64,2176]{1,0:T(8,128)(2,1)S(1)} %collective-permute-done.4.refs_7_), channel_id=1, source_target_pairs={{0,2},{1,3},{2,4},{3,5},{4,6},{5,7},{6,8},{7,9},{8,10},{9,11},{10,... | collective-permute-start | bytes 835592 | tf_op jit(solution)/shard_map/ppermute | solution.py:245
  53.9 0.7 copy-start.7
  54.7 7.8 %collective-permute-start.8 = (bf16[256,2176]{1,0:T(8,128)(2,1)}, bf16[256,2176]{1,0:T(8,128)(2,1)S(1)}, u32[]{:S(2)}, u32[]{:S(2)}) collective-permute-start(bf16[256,2176]{1,0:T(8,128)(2,1)} %shard_map.87.refs_9_), channel_id=1, source_target_pairs={{0,1},{1,0},{2,3},{3,2},{4,5},{5,4},{6,7},{7,6},{8,9},{9,8},{10,11... | collective-permute-start | bytes 3342344 | tf_op jit(solution)/shard_map/ppermute | solution.py:245
  57.6 8.6 %collective-permute-start.10 = (bf16[256,2176]{1,0:T(8,128)(2,1)S(1)}, bf16[256,2176]{1,0:T(8,128)(2,1)S(1)}, u32[]{:S(2)}, u32[]{:S(2)}) collective-permute-start(bf16[256,2176]{1,0:T(8,128)(2,1)S(1)} %collective-permute-done.9.refs_11_), channel_id=1, source_target_pairs={{0,1},{1,0},{2,3},{3,2},{4,5},{5,4},{6,7},{7,6},{8,9},{9,8},{10,11... | collective-permute-start | bytes 3342344 | tf_op jit(solution)/shard_map/ppermute | solution.py:245
  57.7 8.4 %collective-permute-start.6 = (bf16[32,2176]{1,0:T(8,128)(2,1)S(1)}, bf16[32,2176]{1,0:T(8,128)(2,1)S(1)}, u32[]{:S(2)}, u32[]{:S(2)}) collective-permute-start(bf16[32,2176]{1,0:T(8,128)(2,1)S(1)} %slice.8), channel_id=1, source_target_pairs={{0,2},{1,3},{2,4},{3,5},{4,6},{5,7},{6,8},{7,9},{8,10},{9,11},{10,... | collective-permute-start | bytes 417800 | tf_op jit(solution)/shard_map/ppermute | solution.py:245
  58.5 7.6 %collective-permute-start.7 = (bf16[32,2176]{1,0:T(8,128)(2,1)S(1)}, bf16[32,2176]{1,0:T(8,128)(2,1)S(1)}, u32[]{:S(2)}, u32[]{:S(2)}) collective-permute-start(bf16[32,2176]{1,0:T(8,128)(2,1)S(1)} %slice.9), channel_id=1, source_target_pairs={{0,14},{1,15},{2,0},{3,1},{4,2},{5,3},{6,4},{7,5},{8,6},{9,7},{10,... | collective-permute-start | bytes 417800 | tf_op jit(solution)/shard_map/ppermute | solution.py:245
  66.1 1.2 copy-start
  70.0 1.4 copy-start.1
  71.4 1.3 copy-start.3
  72.8 34.1 %copy-start.4 = (s32[3]{0:T(128)S(1)}, s32[3]{0:T(128)}, u32[]{:S(2)}) copy-start(s32[3]{0:T(128)} %pad_add_fusion.place) | copy-start | bytes 40
  72.8 34.1 %all-to-all-start.1 = ((f32[8,64,1024]{2,1,0:T(8,128)}), f32[8,64,1024]{2,1,0:T(8,128)S(1)}, u32[]{:S(2)}, u32[]{:S(2)}) async-start(f32[8,64,1024]{2,1,0:T(8,128)} %copy-done.3), calls=%async_computation.1 | async-start | bytes 4194304 | tf_op jit(solution)/shard_map/all_to_all | solution.py:299
  79.6 69.9 %collective-permute-start.11 = (bf16[512,2176]{1,0:T(8,128)(2,1)}, bf16[512,2176]{1,0:T(8,128)(2,1)}, u32[]{:S(2)}, u32[]{:S(2)}) collective-permute-start(bf16[512,2176]{1,0:T(8,128)(2,1)} %copy-done.1), channel_id=1, source_target_pairs={{0,1},{1,0},{2,3},{3,2},{4,5},{5,4},{6,7},{7,6},{8,9},{9,8},{10,11... | collective-permute-start | bytes 6684680 | tf_op jit(solution)/shard_map/ppermute | solution.py:245
  108.3 11.1 %all-to-all-start.2 = ((f32[8,1,128]{2,1,0:T(1,128)}), f32[8,1,128]{2,1,0:T(1,128)S(1)}, u32[]{:S(2)}, u32[]{:S(2)}) async-start(f32[8,1,128]{2,1,0:T(1,128)} %get-tuple-element.16), calls=%async_computation.2 | async-start | bytes 8192 | tf_op jit(solution)/shard_map/all_to_all | solution.py:311
  121.2 25.6 %all-to-all-start.3 = ((bf16[32,64,256]{2,1,0:T(8,128)(2,1)}), bf16[32,64,256]{2,1,0:T(8,128)(2,1)}, u32[]{:S(2)}, u32[]{:S(2)}) async-start(bf16[32,64,256]{2,1,0:T(8,128)(2,1)} %get-tuple-element.17), calls=%async_computation.3 | async-start | bytes 2097152 | tf_op jit(solution)/shard_map/all_to_all | solution.py:324
  130.5 22.4 %collective-permute-start.13 = (bf16[512,2176]{1,0:T(8,128)(2,1)}, bf16[512,2176]{1,0:T(8,128)(2,1)S(1)}, u32[]{:S(2)}, u32[]{:S(2)}) collective-permute-start(bf16[512,2176]{1,0:T(8,128)(2,1)} %all-gather.2.cloned.1.call-done), channel_id=1, source_target_pairs={{0,1},{1,0},{2,3},{3,2},{4,5},{5,4},{6,7},{7,6},{8,9},{9,8},{10,11... | collective-permute-start | bytes 6684680 | tf_op jit(solution)/shard_map/ppermute | solution.py:245
  146.8 1.9 %copy-start.6 = (bf16[512,2176]{1,0:T(8,128)(2,1)S(1)}, bf16[512,2176]{1,0:T(8,128)(2,1)}, u32[]{:S(2)}) copy-start(bf16[512,2176]{1,0:T(8,128)(2,1)} %all-gather.2.cloned.1.call-done) | copy-start | bytes 6684676
  149.5 2.6 %copy-start.2 = (bf16[512,2176]{1,0:T(8,128)(2,1)S(1)}, bf16[512,2176]{1,0:T(8,128)(2,1)}, u32[]{:S(2)}) copy-start(bf16[512,2176]{1,0:T(8,128)(2,1)} %copy-done.1) | copy-start | bytes 6684676
  152.9 0.8 copy-start.5
Sparse Core Ops, SparseCore 0:
  54.8 41.7 all-gather.1

commit v2 on v1

--- a/solution.py
+++ b/solution.py
@@ -137,16 +137,24 @@
     )(place, references, ctf)
 
 
+def join(blocks, lines):
+    at = 0
+    for block in blocks:
+        lines[at : at + block.shape[0], :] = block[...]
+        at += block.shape[0]
+
+
+def join_kernel(*refs):
+    join(refs[:-1], refs[-1])
+
+
 def score_kernel(counts, *refs):
     count = sum(counts)
     blocks, tables = refs[:count], refs[count : count + 4]
     out, lines = refs[count + 4 :]
     n_dom, rows, width = out.shape[0], out.shape[1], out.shape[2] // 4
     own = rows // len(counts)
-    at = 0
-    for block in blocks:
-        lines[at : at + block.shape[0], :] = block[...]
-        at += block.shape[0]
+    join(blocks, lines)
     share = lines.shape[1] - EXTRA
     extra = lines[:, share:].astype(jnp.float32)
     noise = extra[:, 96:97] + extra[:, 97:98] + extra[:, 98:99]
@@ -168,53 +176,72 @@
 
 
 def soften_kernel(place, parts, score, stats):
+    rows = score.shape[0]
+    own = rows // stats.shape[0]
     value = parts[0]
     for d in range(1, parts.shape[0]):
         value = value + parts[d]
     score[...] = value
-    rows = value.shape[0]
     top = jnp.max(value, axis=1, keepdims=True)
     total = jnp.sum(jnp.exp(value - top), axis=1, keepdims=True)
-    lane, target = places_of(place[1], rows, rows // stats.shape[0])
+    lane, target = places_of(place[1], rows, own)
     both = jnp.where(lane == target, top, 0.0) + jnp.where(lane == target + rows, total, 0.0)
     stats[...] = jnp.broadcast_to(jnp.sum(both, axis=0, keepdims=True)[None], stats.shape)
 
 
-def weigh_kernel(place, score, stats, spread, evidence, table):
-    x_c, z_at = place[0], place[1]
+def weigh_kernel(place, score, stats, spread, evidence):
+    x_c = place[0]
     rows = score.shape[0]
-    own = rows // stats.shape[0]
     tops = stats[...]
     sums = pltpu.roll(tops, rows, 1)
     highest = jnp.max(tops, axis=0, keepdims=True)
     total = jnp.sum(sums * jnp.exp(tops - highest), axis=0, keepdims=True)
     logged = highest + jnp.log(total)
     evidence[...] = logged
-    lane, target = places_of(z_at, rows, own)
+    lane, target = places_of(place[1], rows, rows // stats.shape[0])
     column = jnp.sum(jnp.where(lane == target, logged, 0.0), axis=1, keepdims=True)
-    value = jnp.exp(score[...] - column)
-    for o in range(rows // own):
-        at = pl.multiple_of(lax.rem(z_at + o, rows // own) * own, own)
-        table[pl.ds(at, own), :] = value[o * own : (o + 1) * own, :]
-    width = table.shape[1] // 4
+    value = jnp.exp(score[...] - column).astype(jnp.bfloat16)
+    width = value.shape[1] // 4
     for q in range(4):
-        part = table[:, q * width : (q + 1) * width].astype(jnp.bfloat16)
+        part = value[:, q * width : (q + 1) * width]
         for d in range(spread.shape[0] // 4):
             spread[d * 4 + (q ^ x_c)] = part
 
 
-def divide_kernel(sums, square, regularizer, out):
-    share, width = out.shape
-    n_group = square.shape[1] // 4
-    high = sums[share : share + n_group, :]
-    first = high.astype(jnp.bfloat16).astype(jnp.float32)
+def renew_kernel(place, spread, square, regularizer, *refs):
+    lines, (out, table, weights) = refs[:-3], refs[-3:]
+    x_c = place[0]
+    n_dom, rows, width = spread.shape[0] // 4, spread.shape[1], spread.shape[2]
+    own = 8
+    for q in range(4):
+        for d in range(n_dom):
+            value = spread[d * 4 + (q ^ x_c)].astype(jnp.float32)
+            for o in range(rows // own):
+                at = (o * n_dom + d) * own
+                table[at : at + own, :] = value[o * own : (o + 1) * own, :]
+        weights[q * n_dom * rows : (q + 1) * n_dom * rows, :] = table[...].astype(jnp.bfloat16)
+
+    def product(first, span):
+        total = jnp.zeros((span, width), jnp.float32)
+        at = 0
+        for some in lines:
+            total = total + lax.dot_general(
+                some[:, first : first + span], weights[at : at + some.shape[0], :], (((0,), (0,)), ((), ())), preferred_element_type=jnp.float32
+            )
+            at += some.shape[0]
+        return total
+
+    share = out.shape[0]
+    group = square.shape[1] // 4
+    high = product(share, EXTRA)[:group]
+    first = rounded(high)
     second = (high - first).astype(jnp.bfloat16)
     first = first.astype(jnp.bfloat16)
     factors = jnp.concatenate([first, first, second, jnp.zeros_like(second)], axis=0)
     step = 256
     for at in range(0, share, step):
         bottom = jnp.dot(square[at : at + step, :], factors, preferred_element_type=jnp.float32)
-        out[at : at + step, :] = sums[at : at + step, :] / (bottom + regularizer[...])
+        out[at : at + step, :] = product(at, step) / (bottom + regularizer[...])
 
 
 def ring_tables(mesh):
@@ -257,6 +284,7 @@
 
     pieces = filtered_shares(particles, offsets, groups, precision, ctf, n_dom)
 
+    rows = depth * own
     place = jnp.stack([x_at * 2 + c_at, z_at, dom])
     table = share_table(lax.optimization_barrier((place, pieces))[0], references, ctf, n_dom)
     ctf_share = lax.dynamic_slice_in_dim(ctf, dom * share, share, 1)
@@ -268,22 +296,21 @@
     block = lax.all_to_all(pieces, "dom", 0, 0, tiled=True)
     block = block.reshape(n_dom * own, share + EXTRA)
     half = block.shape[0] // 2
-    table_x = send("side", table)
+    table_x = send("side", lax.optimization_barrier((table, block))[0])
     beside = send("side", block)
 
+    up = [block[:half], block[half:]]
+    down = list(up)
     held = {0: [block]}
-    up = down = block
     for step in range(1, depth // 2):
-        up, down = send("up", up), send("down", down)
-        held[depth - step] = [up]
-        held[step] = [down]
-    table_x = lax.optimization_barrier((table_x, up, down))[0]
-    beside = lax.optimization_barrier((beside, up, down))[0]
-    held[depth // 2] = [send("up", up[:half]), send("down", down[half:])]
-    beside = lax.all_gather(beside, "ref", axis=0, tiled=True, axis_index_groups=tables["column"])
+        for h in range(2):
+            sent = (send("up", up[h]), send("down", down[h]))
+            up[h], down[h] = lax.optimization_barrier(sent + (up[1 - h], down[1 - h]))[:2]
+        held[depth - step] = list(up)
+        held[step] = list(down)
+    table_x = lax.optimization_barrier((table_x, up[1], down[1]))[0]
+    held[depth // 2] = [send("up", up[0]), send("down", down[1])]
     tables4 = [table, send("core", table), table_x, send("core", table_x)]
-
-    rows = depth * own
     blocks = [held[o] for o in range(depth)]
     counts = [len(v) for v in blocks]
     parts, mine = pl.pallas_call(
@@ -296,7 +323,24 @@
         out_specs=(VMEM, VMEM),
         compiler_params=ROOM,
     )(*[v for some in blocks for v in some], *tables4)
+    beside, parts = lax.optimization_barrier((beside, parts))
     parts = lax.all_to_all(parts, "dom", 0, 0, tiled=True)
+
+    up = down = beside
+    found = {0: [beside]}
+    for step in range(1, depth // 2):
+        up, down = send("up", up), send("down", down)
+        found[depth - step] = [up]
+        found[step] = [down]
+    found[depth // 2] = [send("up", up[:half]), send("down", down[half:])]
+    found = [v for o in range(depth) for v in found[o]]
+    beside = pl.pallas_call(
+        join_kernel,
+        out_shape=jax.ShapeDtypeStruct((n_dom * rows, share + EXTRA), beside.dtype),
+        in_specs=[VMEM] * len(found),
+        out_specs=VMEM,
+        compiler_params=ROOM,
+    )(*found)
 
     score, stats = pl.pallas_call(
         soften_kernel,
@@ -317,37 +361,24 @@
         ),
         in_specs=[SMEM, VMEM, VMEM],
         out_specs=(VMEM, VMEM),
-        scratch_shapes=[pltpu.VMEM((rows, 4 * n_own_ref), jnp.float32)],
         compiler_params=ROOM,
     )(place, score, stats.reshape(depth, 2 * rows))
     log_evidence = lax.dynamic_slice(evidence, (0, z_at * own), (1, own)).reshape(own)
     weights = lax.all_to_all(
         weights, ("dom", "ref"), 0, 0, tiled=True, axis_index_groups=tables["same_z"]
     )
-    weights = weights.reshape(n_dom, 2, 2, depth, own, n_own_ref)
-
-    def order(x, c, turn):
-        some = lax.dynamic_slice(
-            weights, (0, x, c, 0, 0, 0), (n_dom, 1, 1, depth, own, n_own_ref)
-        ).reshape(n_dom, depth, own, n_own_ref)
-        if turn:
-            some = lax.dynamic_slice_in_dim(jnp.concatenate([some, some], axis=1), z_at, depth, 1)
-        return some.transpose(1, 0, 2, 3).reshape(-1, n_own_ref)
-
-    sums = 0.0
-    for some, side in ((mine, 0), (beside, 1)):
-        for rows_of, core in ((some, 0), (send("core", some), 1)):
-            weight = order((x_at + side) % 2, (c_at + core) % 2, side == 0)
-            sums = sums + lax.dot_general(
-                rows_of, weight, (((0,), (0,)), ((), ())), preferred_element_type=jnp.float32
-            )
+    lines = [mine, send("core", mine), beside, send("core", beside)]
     new_references = pl.pallas_call(
-        divide_kernel,
+        renew_kernel,
         out_shape=jax.ShapeDtypeStruct((share, n_own_ref), jnp.float32),
-        in_specs=[VMEM, VMEM, VMEM],
+        in_specs=[SMEM] + [VMEM] * (3 + len(lines)),
         out_specs=VMEM,
+        scratch_shapes=[
+            pltpu.VMEM((n_dom * rows, n_own_ref), jnp.float32),
+            pltpu.VMEM((4 * n_dom * rows, n_own_ref), jnp.bfloat16),
+        ],
         compiler_params=ROOM,
-    )(sums, square, regularizer[None, :])
+    )(place, weights, square, regularizer[None, :], *lines)
     return new_references, log_evidence
 
 

time: 163 us -> 146 us (0.90)
  waiting for transfers between devices: 66.7 us -> 43.8 us
  starting transfers between devices: 49.5 us -> 69.4 us
  between operations: 14.4 us -> 0.82 us
  Pallas kernels: 14.7 us -> 22 us
  matrix products: 4.96 us -> 0 us
  local copies, waits for them, and re-layouts: 8.35 us -> 6.29 us
    all_to_all x1, waiting for transfers between devices: 26.1 us -> 0.95 us  [local(): parts = lax.all_to_all(parts, 'dom', 0, 0, tiled=True)]
    ppermute x14 -> x28, starting transfers between devices: 22.2 us -> 46.8 us  [send(): return lax.ppermute(value, axis, pairs)]
    pallas_call x1 -> x2, Pallas kernels: 1.74 us -> 7.24 us  [the longest x1 7.09 us: local(): pl.pallas_call(renew_kernel, out_shape=jax.ShapeDtypeStruct((share, n_own...]
    dot_general x4 -> x0, matrix products: 4.96 us -> none  [local(): lax.dot_general(rows_of, weight, (((0,), (0,)), ((), ())), preferred_elem...]
    all_to_all x1, starting transfers between devices: 6.87 us -> 4.35 us  [local(): parts = lax.all_to_all(parts, 'dom', 0, 0, tiled=True)]
    ppermute x14 -> x28, waiting for transfers between devices: 19.4 us -> 21.8 us  [send(): return lax.ppermute(value, axis, pairs)]
    pallas_call x1, Pallas kernels: 2.64 us -> 4.36 us  [local(): pl.pallas_call(functools.partial(score_kernel, counts), out_shape=(jax.Sh...]
    unnamed x17 -> x13, local copies, waits for them, and re-layouts: 5.19 us -> 4.61 us
  transfers between devices with their start and end apart: 19 -> 32, of which waited for: 8 -> 14; matrix products, arithmetic and copies ran while one was open for 7% -> 4% of each run, Pallas kernels for 6% -> 8%
where the time goes in v2:
time: 146 us
  starting transfers between devices  69.4 us (48%)
  waiting for transfers between devices  43.8 us (30%)
  Pallas kernels  22 us (15%)
  local copies, waits for them, and re-layouts  6.29 us (4%)
  other arithmetic  3.38 us (2%)
    ppermute x28, starting transfers between devices, send(): return lax.ppermute(value, axis, pairs)  46.8 us
    ppermute x28, waiting for transfers between devices, send(): return lax.ppermute(value, axis, pairs)  21.8 us
    all_to_all x1, waiting for transfers between devices, local(): lax.all_to_all(weights, ('dom', 'ref'), 0, 0, tiled=True, axis_index_grou...  14 us
    all_to_all x1, starting transfers between devices, local(): block = lax.all_to_all(pieces, 'dom', 0, 0, tiled=True)  7.49 us
    all_to_all x1, starting transfers between devices, local(): lax.all_to_all(weights, ('dom', 'ref'), 0, 0, tiled=True, axis_index_grou...  7.22 us
    pallas_call x1, Pallas kernels, local(): pl.pallas_call(renew_kernel, out_shape=jax.ShapeDtypeStruct((share, n_own...  7.09 us
    unnamed x13, local copies, waits for them, and re-layouts  4.61 us
    pallas_call x1, Pallas kernels, local(): pl.pallas_call(functools.partial(score_kernel, counts), out_shape=(jax.Sh...  4.36 us
  transfers between devices with their start and end apart: 32, of which 14 were waited for; matrix products, arithmetic and copies ran while one was open for 4% of the time, Pallas kernels for 8%

profile of v2, /device:TPU:1, one launch (start us, length us, event | category | flops | bytes accessed | tf_op | source)
XLA Modules:
  0.0 145.7 jit_solution(13078036602492167008)
XLA Ops:
  0.6 3.3 %shard_map.86 = bf16[8,8,2176]{2,1,0:T(8,128)(2,1)} custom-call(s32[2,8]{1,0:T(2,128)} %bitcast.20, s32[8]{0:T(128)} %groups.1, f32[8]{0:T(128)} %precision.1, bf16[8,16384]{1,0:T(8,128)(2,1)} %particles.1, f32[32,16384]{1,0:T(8,128)} %ctf.3), custom_call_target="tpu_custom_call" | custom-call | tf_op jit(solution)/shard_map/pallas_call | solution.py:76
  3.9 7.5 %all-to-all-start = ((bf16[8,8,2176]{2,1,0:T(8,128)(2,1)}), bf16[8,8,2176]{2,1,0:T(8,128)(2,1)S(1)}, u32[]{:S(2)}, u32[]{:S(2)}) async-start(bf16[8,8,2176]{2,1,0:T(8,128)(2,1)} %shard_map.86), calls=%async_computation | async-start | bytes 557056 | tf_op jit(solution)/shard_map/all_to_all | solution.py:296
  11.4 0.7 pad_add_fusion.place
  12.1 3.9 %shard_map.87.refs_15_ = bf16[256,2176]{1,0:T(8,128)(2,1)} custom-call(s32[3]{0:T(128)} %pad_add_fusion.place, bf16[256,16384]{1,0:T(8,128)(2,1)} %references.1, f32[32,16384]{1,0:T(8,128)} %ctf.3), custom_call_target="tpu_custom_call" | custom-call | flops 536870912 | bytes 8388608 | tf_op jit(solution)/shard_map/pallas_call | solution.py:125
  15.9 3.2 %all-to-all-done = bf16[8,8,2176]{2,1,0:T(8,128)(2,1)S(1)} async-done(((bf16[8,8,2176]{2,1,0:T(8,128)(2,1)}), bf16[8,8,2176]{2,1,0:T(8,128)(2,1)S(1)}, u32[]{:S(2)}, u32[]{:S(2)}) %all-to-all-start) | async-done | bytes 278560 | tf_op jit(solution)/shard_map/all_to_all | solution.py:296
  19.1 0.3 collective-permute-start.16
  19.5 5.7 %collective-permute-start.2 = (bf16[32,2176]{1,0:T(8,128)(2,1)S(1)}, bf16[32,2176]{1,0:T(8,128)(2,1)S(1)}, u32[]{:S(2)}, u32[]{:S(2)}) collective-permute-start(bf16[32,2176]{1,0:T(8,128)(2,1)S(1)} %get-tuple-element.51), channel_id=1, source_target_pairs={{0,14},{1,15},{2,0},{3,1},{4,2},{5,3},{6,4},{7,5},{8,6},{9,7},{10,... | collective-permute-start | bytes 417800 | tf_op jit(solution)/shard_map/ppermute | solution.py:272
  25.1 2.7 %collective-permute-start.4 = (bf16[32,2176]{1,0:T(8,128)(2,1)S(1)}, bf16[32,2176]{1,0:T(8,128)(2,1)S(1)}, u32[]{:S(2)}, u32[]{:S(2)}) collective-permute-start(bf16[32,2176]{1,0:T(8,128)(2,1)S(1)} %get-tuple-element.50), channel_id=1, source_target_pairs={{0,14},{1,15},{2,0},{3,1},{4,2},{5,3},{6,4},{7,5},{8,6},{9,7},{10,... | collective-permute-start | bytes 417800 | tf_op jit(solution)/shard_map/ppermute | solution.py:272
  27.8 0.0 collective-permute-start.3
  27.8 0.0 collective-permute-done.2.refs_1_
  27.8 2.4 %collective-permute-done.1.refs_13_ = bf16[32,2176]{1,0:T(8,128)(2,1)S(1)} collective-permute-done((bf16[32,2176]{1,0:T(8,128)(2,1)S(1)}, bf16[32,2176]{1,0:T(8,128)(2,1)S(1)}, u32[]{:S(2)}, u32[]{:S(2)}) %collective-permute-start.1) | collective-permute-done | bytes 139296 | tf_op jit(solution)/shard_map/ppermute | solution.py:272
  30.3 0.2 collective-permute-start.6
  30.5 1.2 collective-permute-start.5
  31.7 0.0 collective-permute-done.4.refs_2_
  31.7 2.6 %collective-permute-done.3.refs_14_ = bf16[32,2176]{1,0:T(8,128)(2,1)S(1)} collective-permute-done((bf16[32,2176]{1,0:T(8,128)(2,1)S(1)}, bf16[32,2176]{1,0:T(8,128)(2,1)S(1)}, u32[]{:S(2)}, u32[]{:S(2)}) %collective-permute-start.3) | collective-permute-done | bytes 139296 | tf_op jit(solution)/shard_map/ppermute | solution.py:272
  34.3 0.2 collective-permute-start.8
  34.5 1.3 collective-permute-start.7
  35.8 1.2 collective-permute-done.5.refs_11_
  36.9 0.2 collective-permute-start.10
  37.2 1.2 collective-permute-start.9
  38.4 0.1 collective-permute-done.8.refs_4_
  38.5 1.1 collective-permute-done.7.refs_12_
  39.6 0.5 collective-permute-start.12
  40.1 1.0 collective-permute-start.11
  41.1 0.6 collective-permute-done.10.refs_5_
  41.7 6.3 %collective-permute-start.15 = (bf16[256,2176]{1,0:T(8,128)(2,1)}, bf16[256,2176]{1,0:T(8,128)(2,1)S(1)}, u32[]{:S(2)}, u32[]{:S(2)}) collective-permute-start(bf16[256,2176]{1,0:T(8,128)(2,1)} %shard_map.87.refs_15_), channel_id=1, source_target_pairs={{0,1},{1,0},{2,3},{3,2},{4,5},{5,4},{6,7},{7,6},{8,9},{9,8},{10,11... | collective-permute-start | bytes 3342344 | tf_op jit(solution)/shard_map/ppermute | solution.py:272
  48.0 4.2 %collective-permute-start.17 = (bf16[256,2176]{1,0:T(8,128)(2,1)S(1)}, bf16[256,2176]{1,0:T(8,128)(2,1)S(1)}, u32[]{:S(2)}, u32[]{:S(2)}) collective-permute-start(bf16[256,2176]{1,0:T(8,128)(2,1)S(1)} %collective-permute-done.16.refs_17_), channel_id=1, source_target_pairs={{0,1},{1,0},{2,3},{3,2},{4,5},{5,4},{6,7},{7,6},{8,9},{9,8},{10,11... | collective-permute-start | bytes 3342344 | tf_op jit(solution)/shard_map/ppermute | solution.py:272
  52.2 1.2 collective-permute-start
  53.3 0.5 collective-permute-start.13
  53.9 2.1 %collective-permute-start.14 = (bf16[32,2176]{1,0:T(8,128)(2,1)S(1)}, bf16[32,2176]{1,0:T(8,128)(2,1)S(1)}, u32[]{:S(2)}, u32[]{:S(2)}) collective-permute-start(bf16[32,2176]{1,0:T(8,128)(2,1)S(1)} %collective-permute-done.12.refs_6_), channel_id=1, source_target_pairs={{0,14},{1,15},{2,0},{3,1},{4,2},{5,3},{6,4},{7,5},{8,6},{9,7},{10,... | collective-permute-start | bytes 417800 | tf_op jit(solution)/shard_map/ppermute | solution.py:272
  56.0 3.5 %collective-permute-done.13.refs_7_ = bf16[32,2176]{1,0:T(8,128)(2,1)S(1)} collective-permute-done((bf16[32,2176]{1,0:T(8,128)(2,1)S(1)}, bf16[32,2176]{1,0:T(8,128)(2,1)S(1)}, u32[]{:S(2)}, u32[]{:S(2)}) %collective-permute-start.13) | collective-permute-done | bytes 139296 | tf_op jit(solution)/shard_map/ppermute | solution.py:272
  59.5 0.0 copy-start
  59.6 1.2 copy-done
  60.8 4.4 %shard_map.88 = (f32[8,64,1024]{2,1,0:T(8,128)}, bf16[512,2176]{1,0:T(8,128)(2,1)}) custom-call(bf16[64,2176]{1,0:T(8,128)(2,1)S(1)} %bitcast.17, bf16[32,2176]{1,0:T(8,128)(2,1)S(1)} %collective-permute-done.2.refs_1_, bf16[32,2176]{1,0:T(8,128)(2,1)S(1)} %collective-permute-done.4.refs_2_, bf16[32,2176]{1,0:T(8,128)(2,1)S(1)} %collective-permute-done.6.refs_3_, ...), custom_call_target="tpu_custom_call" | custom-call | tf_op jit(solution)/shard_map/pallas_call | solution.py:316
  65.2 2.7 %collective-permute-start.19 = (bf16[64,2176]{1,0:T(8,128)(2,1)S(1)}, bf16[64,2176]{1,0:T(8,128)(2,1)S(1)}, u32[]{:S(2)}, u32[]{:S(2)}) collective-permute-start(bf16[64,2176]{1,0:T(8,128)(2,1)S(1)} %collective-permute-done.refs_0_), channel_id=1, source_target_pairs={{0,14},{1,15},{2,0},{3,1},{4,2},{5,3},{6,4},{7,5},{8,6},{9,7},{10,... | collective-permute-start | bytes 835592 | tf_op jit(solution)/shard_map/ppermute | solution.py:272
  67.8 4.3 %all-to-all-start.1 = ((f32[8,64,1024]{2,1,0:T(8,128)}), f32[8,64,1024]{2,1,0:T(8,128)}, u32[]{:S(2)}, u32[]{:S(2)}) async-start(f32[8,64,1024]{2,1,0:T(8,128)} %get-tuple-element.41), calls=%async_computation.1 | async-start | bytes 4194304 | tf_op jit(solution)/shard_map/all_to_all | solution.py:327
  72.2 1.2 collective-permute-done.22.refs_8_
  73.4 2.7 %collective-permute-start.20 = (bf16[64,2176]{1,0:T(8,128)(2,1)S(1)}, bf16[64,2176]{1,0:T(8,128)(2,1)S(1)}, u32[]{:S(2)}, u32[]{:S(2)}) collective-permute-start(bf16[64,2176]{1,0:T(8,128)(2,1)S(1)} %collective-permute-done.19.refs_1_), channel_id=1, source_target_pairs={{0,14},{1,15},{2,0},{3,1},{4,2},{5,3},{6,4},{7,5},{8,6},{9,7},{10,... | collective-permute-start | bytes 835592 | tf_op jit(solution)/shard_map/ppermute | solution.py:272
  76.1 4.8 %collective-permute-done.23.refs_7_ = bf16[64,2176]{1,0:T(8,128)(2,1)S(1)} collective-permute-done((bf16[64,2176]{1,0:T(8,128)(2,1)S(1)}, bf16[64,2176]{1,0:T(8,128)(2,1)S(1)}, u32[]{:S(2)}, u32[]{:S(2)}) %collective-permute-start.23) | collective-permute-done | bytes 278560 | tf_op jit(solution)/shard_map/ppermute | solution.py:272
  80.9 2.7 %collective-permute-start.21 = (bf16[64,2176]{1,0:T(8,128)(2,1)S(1)}, bf16[64,2176]{1,0:T(8,128)(2,1)S(1)}, u32[]{:S(2)}, u32[]{:S(2)}) collective-permute-start(bf16[64,2176]{1,0:T(8,128)(2,1)S(1)} %collective-permute-done.20.refs_2_), channel_id=1, source_target_pairs={{0,14},{1,15},{2,0},{3,1},{4,2},{5,3},{6,4},{7,5},{8,6},{9,7},{10,... | collective-permute-start | bytes 835592 | tf_op jit(solution)/shard_map/ppermute | solution.py:272
  83.5 4.3 %collective-permute-done.24.refs_6_ = bf16[64,2176]{1,0:T(8,128)(2,1)S(1)} collective-permute-done((bf16[64,2176]{1,0:T(8,128)(2,1)S(1)}, bf16[64,2176]{1,0:T(8,128)(2,1)S(1)}, u32[]{:S(2)}, u32[]{:S(2)}) %collective-permute-start.24) | collective-permute-done | bytes 278560 | tf_op jit(solution)/shard_map/ppermute | solution.py:272
  87.9 0.1 collective-permute-start.25
  88.0 2.7 %collective-permute-start.26 = (bf16[32,2176]{1,0:T(8,128)(2,1)S(1)}, bf16[32,2176]{1,0:T(8,128)(2,1)S(1)}, u32[]{:S(2)}, u32[]{:S(2)}) collective-permute-start(bf16[32,2176]{1,0:T(8,128)(2,1)S(1)} %slice.27), channel_id=1, source_target_pairs={{0,14},{1,15},{2,0},{3,1},{4,2},{5,3},{6,4},{7,5},{8,6},{9,7},{10,... | collective-permute-start | bytes 417800 | tf_op jit(solution)/shard_map/ppermute | solution.py:272
  90.7 4.2 %collective-permute-start.18 = (bf16[512,2176]{1,0:T(8,128)(2,1)}, bf16[512,2176]{1,0:T(8,128)(2,1)}, u32[]{:S(2)}, u32[]{:S(2)}) collective-permute-start(bf16[512,2176]{1,0:T(8,128)(2,1)} %get-tuple-element.45.refs_0_), channel_id=1, source_target_pairs={{0,1},{1,0},{2,3},{3,2},{4,5},{5,4},{6,7},{7,6},{8,9},{9,8},{10,11... | collective-permute-start | bytes 6684680 | tf_op jit(solution)/shard_map/ppermute | solution.py:272
  94.9 0.2 shard_map.91.refs_2_
  95.1 3.0 %collective-permute-start.27 = (bf16[512,2176]{1,0:T(8,128)(2,1)S(1)}, bf16[512,2176]{1,0:T(8,128)(2,1)}, u32[]{:S(2)}, u32[]{:S(2)}) collective-permute-start(bf16[512,2176]{1,0:T(8,128)(2,1)S(1)} %shard_map.91.refs_2_), channel_id=1, source_target_pairs={{0,1},{1,0},{2,3},{3,2},{4,5},{5,4},{6,7},{7,6},{8,9},{9,8},{10,11... | collective-permute-start | bytes 6684680 | tf_op jit(solution)/shard_map/ppermute | solution.py:272
  98.1 0.9 all-to-all-done.1.parts
  99.0 2.5 %shard_map.89 = (f32[64,1024]{1,0:T(8,128)S(1)}, f32[8,1,128]{2,1,0:T(1,128)}) custom-call(s32[3]{0:T(128)S(1)} %copy-done.3, f32[8,64,1024]{2,1,0:T(8,128)} %all-to-all-done.1.parts), custom_call_target="tpu_custom_call" | custom-call | tf_op jit(solution)/shard_map/pallas_call | solution.py:345
  101.5 3.5 %all-to-all-start.2 = ((f32[8,1,128]{2,1,0:T(1,128)}), f32[8,1,128]{2,1,0:T(1,128)S(1)}, u32[]{:S(2)}, u32[]{:S(2)}) async-start(f32[8,1,128]{2,1,0:T(1,128)} %get-tuple-element.43), calls=%async_computation.2 | async-start | bytes 8192 | tf_op jit(solution)/shard_map/all_to_all | solution.py:355
  105.0 1.0 constant_dynamic-slice_fusion
  106.0 1.4 copy.13
  107.4 0.1 pad.3.clone
  107.4 3.9 %all-to-all-done.2 = f32[8,1,128]{2,1,0:T(1,128)S(1)} async-done(((f32[8,1,128]{2,1,0:T(1,128)}), f32[8,1,128]{2,1,0:T(1,128)S(1)}, u32[]{:S(2)}, u32[]{:S(2)}) %all-to-all-start.2) | async-done | bytes 4128 | tf_op jit(solution)/shard_map/all_to_all | solution.py:355
  111.3 0.8 shard_map.90
  112.1 0.0 copy-start.2
  112.1 1.0 copy-done.2
  113.1 7.2 %all-to-all-start.3 = ((bf16[32,64,256]{2,1,0:T(8,128)(2,1)}), bf16[32,64,256]{2,1,0:T(8,128)(2,1)S(1)}, u32[]{:S(2)}, u32[]{:S(2)}) async-start(bf16[32,64,256]{2,1,0:T(8,128)(2,1)} %copy-done.2), calls=%async_computation.3 | async-start | bytes 2097152 | tf_op jit(solution)/shard_map/all_to_all | solution.py:367
  120.3 0.0 copy-start.5
  120.3 1.4 fusion
  121.8 1.3 maximum_maximum_fusion.square
  123.1 0.6 dynamic-slice_bitcast_fusion
  123.6 14.0 %all-to-all-done.3.spread = bf16[32,64,256]{2,1,0:T(8,128)(2,1)S(1)} async-done(((bf16[32,64,256]{2,1,0:T(8,128)(2,1)}), bf16[32,64,256]{2,1,0:T(8,128)(2,1)S(1)}, u32[]{:S(2)}, u32[]{:S(2)}) %all-to-all-start.3) | async-done | bytes 1048608 | tf_op jit(solution)/shard_map/all_to_all | solution.py:367
  137.6 1.0 copy-done.1
  138.7 7.1 %shard_map.92 = f32[2048,256]{1,0:T(8,128)} custom-call(s32[3]{0:T(128)S(1)} %copy-done.4, bf16[32,64,256]{2,1,0:T(8,128)(2,1)S(1)} %all-to-all-done.3.spread, bf16[2048,128]{1,0:T(8,128)(2,1)S(1)} %copy-done.1, f32[1,256]{1,0:T(1,128)S(1)} %bitcast.19, bf16[512,2176]{1,0:T(8,128)(2,1)} %get-tuple-element.45.refs_0_, ...), custom_call_target="tpu_custom_call" | custom-call | tf_op jit(solution)/shard_map/pallas_call | solution.py:371
  (30 shorter events, 0.1 us)
Async XLA Ops:
  3.9 15.2 %all-to-all-start = ((bf16[8,8,2176]{2,1,0:T(8,128)(2,1)}), bf16[8,8,2176]{2,1,0:T(8,128)(2,1)S(1)}, u32[]{:S(2)}, u32[]{:S(2)}) async-start(bf16[8,8,2176]{2,1,0:T(8,128)(2,1)} %shard_map.86), calls=%async_computation | async-start | bytes 557056 | tf_op jit(solution)/shard_map/all_to_all | solution.py:296
  19.1 28.8 %collective-permute-start.16 = (bf16[256,2176]{1,0:T(8,128)(2,1)}, bf16[256,2176]{1,0:T(8,128)(2,1)S(1)}, u32[]{:S(2)}, u32[]{:S(2)}) collective-permute-start(bf16[256,2176]{1,0:T(8,128)(2,1)} %shard_map.87.refs_15_), channel_id=1, source_target_pairs={{0,16},{1,17},{2,18},{3,19},{4,20},{5,21},{6,22},{7,23},{8,24},{9,... | collective-permute-start | bytes 3342344 | tf_op jit(solution)/shard_map/ppermute | solution.py:272
  19.5 8.3 %collective-permute-start.2 = (bf16[32,2176]{1,0:T(8,128)(2,1)S(1)}, bf16[32,2176]{1,0:T(8,128)(2,1)S(1)}, u32[]{:S(2)}, u32[]{:S(2)}) collective-permute-start(bf16[32,2176]{1,0:T(8,128)(2,1)S(1)} %get-tuple-element.51), channel_id=1, source_target_pairs={{0,14},{1,15},{2,0},{3,1},{4,2},{5,3},{6,4},{7,5},{8,6},{9,7},{10,... | collective-permute-start | bytes 417800 | tf_op jit(solution)/shard_map/ppermute | solution.py:272
  25.1 5.1 %collective-permute-start.1 = (bf16[32,2176]{1,0:T(8,128)(2,1)S(1)}, bf16[32,2176]{1,0:T(8,128)(2,1)S(1)}, u32[]{:S(2)}, u32[]{:S(2)}) collective-permute-start(bf16[32,2176]{1,0:T(8,128)(2,1)S(1)} %get-tuple-element.51), channel_id=1, source_target_pairs={{0,2},{1,3},{2,4},{3,5},{4,6},{5,7},{6,8},{7,9},{8,10},{9,11},{10,... | collective-permute-start | bytes 417800 | tf_op jit(solution)/shard_map/ppermute | solution.py:272
  25.1 6.6 %collective-permute-start.4 = (bf16[32,2176]{1,0:T(8,128)(2,1)S(1)}, bf16[32,2176]{1,0:T(8,128)(2,1)S(1)}, u32[]{:S(2)}, u32[]{:S(2)}) collective-permute-start(bf16[32,2176]{1,0:T(8,128)(2,1)S(1)} %get-tuple-element.50), channel_id=1, source_target_pairs={{0,14},{1,15},{2,0},{3,1},{4,2},{5,3},{6,4},{7,5},{8,6},{9,7},{10,... | collective-permute-start | bytes 417800 | tf_op jit(solution)/shard_map/ppermute | solution.py:272
  27.8 6.5 %collective-permute-start.3 = (bf16[32,2176]{1,0:T(8,128)(2,1)S(1)}, bf16[32,2176]{1,0:T(8,128)(2,1)S(1)}, u32[]{:S(2)}, u32[]{:S(2)}) collective-permute-start(bf16[32,2176]{1,0:T(8,128)(2,1)S(1)} %get-tuple-element.50), channel_id=1, source_target_pairs={{0,2},{1,3},{2,4},{3,5},{4,6},{5,7},{6,8},{7,9},{8,10},{9,11},{10,... | collective-permute-start | bytes 417800 | tf_op jit(solution)/shard_map/ppermute | solution.py:272
  30.3 5.5 %collective-permute-start.6 = (bf16[32,2176]{1,0:T(8,128)(2,1)S(1)}, bf16[32,2176]{1,0:T(8,128)(2,1)S(1)}, u32[]{:S(2)}, u32[]{:S(2)}) collective-permute-start(bf16[32,2176]{1,0:T(8,128)(2,1)S(1)} %collective-permute-done.2.refs_1_), channel_id=1, source_target_pairs={{0,14},{1,15},{2,0},{3,1},{4,2},{5,3},{6,4},{7,5},{8,6},{9,7},{10,... | collective-permute-start | bytes 417800 | tf_op jit(solution)/shard_map/ppermute | solution.py:272
  30.5 6.4 %collective-permute-start.5 = (bf16[32,2176]{1,0:T(8,128)(2,1)S(1)}, bf16[32,2176]{1,0:T(8,128)(2,1)S(1)}, u32[]{:S(2)}, u32[]{:S(2)}) collective-permute-start(bf16[32,2176]{1,0:T(8,128)(2,1)S(1)} %collective-permute-done.1.refs_13_), channel_id=1, source_target_pairs={{0,2},{1,3},{2,4},{3,5},{4,6},{5,7},{6,8},{7,9},{8,10},{9,11},{10,... | collective-permute-start | bytes 417800 | tf_op jit(solution)/shard_map/ppermute | solution.py:272
  34.3 4.2 %collective-permute-start.8 = (bf16[32,2176]{1,0:T(8,128)(2,1)S(1)}, bf16[32,2176]{1,0:T(8,128)(2,1)S(1)}, u32[]{:S(2)}, u32[]{:S(2)}) collective-permute-start(bf16[32,2176]{1,0:T(8,128)(2,1)S(1)} %collective-permute-done.4.refs_2_), channel_id=1, source_target_pairs={{0,14},{1,15},{2,0},{3,1},{4,2},{5,3},{6,4},{7,5},{8,6},{9,7},{10,... | collective-permute-start | bytes 417800 | tf_op jit(solution)/shard_map/ppermute | solution.py:272
  34.5 5.1 %collective-permute-start.7 = (bf16[32,2176]{1,0:T(8,128)(2,1)S(1)}, bf16[32,2176]{1,0:T(8,128)(2,1)S(1)}, u32[]{:S(2)}, u32[]{:S(2)}) collective-permute-start(bf16[32,2176]{1,0:T(8,128)(2,1)S(1)} %collective-permute-done.3.refs_14_), channel_id=1, source_target_pairs={{0,2},{1,3},{2,4},{3,5},{4,6},{5,7},{6,8},{7,9},{8,10},{9,11},{10,... | collective-permute-start | bytes 417800 | tf_op jit(solution)/shard_map/ppermute | solution.py:272
  36.9 4.7 %collective-permute-start.10 = (bf16[32,2176]{1,0:T(8,128)(2,1)S(1)}, bf16[32,2176]{1,0:T(8,128)(2,1)S(1)}, u32[]{:S(2)}, u32[]{:S(2)}) collective-permute-start(bf16[32,2176]{1,0:T(8,128)(2,1)S(1)} %collective-permute-done.6.refs_3_), channel_id=1, source_target_pairs={{0,14},{1,15},{2,0},{3,1},{4,2},{5,3},{6,4},{7,5},{8,6},{9,7},{10,... | collective-permute-start | bytes 417800 | tf_op jit(solution)/shard_map/ppermute | solution.py:272
  37.2 10.8 %collective-permute-start.9 = (bf16[32,2176]{1,0:T(8,128)(2,1)S(1)}, bf16[32,2176]{1,0:T(8,128)(2,1)S(1)}, u32[]{:S(2)}, u32[]{:S(2)}) collective-permute-start(bf16[32,2176]{1,0:T(8,128)(2,1)S(1)} %collective-permute-done.5.refs_11_), channel_id=1, source_target_pairs={{0,2},{1,3},{2,4},{3,5},{4,6},{5,7},{6,8},{7,9},{8,10},{9,11},{10,... | collective-permute-start | bytes 417800 | tf_op jit(solution)/shard_map/ppermute | solution.py:272
  39.6 8.3 %collective-permute-start.12 = (bf16[32,2176]{1,0:T(8,128)(2,1)S(1)}, bf16[32,2176]{1,0:T(8,128)(2,1)S(1)}, u32[]{:S(2)}, u32[]{:S(2)}) collective-permute-start(bf16[32,2176]{1,0:T(8,128)(2,1)S(1)} %collective-permute-done.8.refs_4_), channel_id=1, source_target_pairs={{0,14},{1,15},{2,0},{3,1},{4,2},{5,3},{6,4},{7,5},{8,6},{9,7},{10,... | collective-permute-start | bytes 417800 | tf_op jit(solution)/shard_map/ppermute | solution.py:272
  40.1 7.9 %collective-permute-start.11 = (bf16[32,2176]{1,0:T(8,128)(2,1)S(1)}, bf16[32,2176]{1,0:T(8,128)(2,1)S(1)}, u32[]{:S(2)}, u32[]{:S(2)}) collective-permute-start(bf16[32,2176]{1,0:T(8,128)(2,1)S(1)} %collective-permute-done.7.refs_12_), channel_id=1, source_target_pairs={{0,2},{1,3},{2,4},{3,5},{4,6},{5,7},{6,8},{7,9},{8,10},{9,11},{10,... | collective-permute-start | bytes 417800 | tf_op jit(solution)/shard_map/ppermute | solution.py:272
  41.7 17.9 %collective-permute-start.15 = (bf16[256,2176]{1,0:T(8,128)(2,1)}, bf16[256,2176]{1,0:T(8,128)(2,1)S(1)}, u32[]{:S(2)}, u32[]{:S(2)}) collective-permute-start(bf16[256,2176]{1,0:T(8,128)(2,1)} %shard_map.87.refs_15_), channel_id=1, source_target_pairs={{0,1},{1,0},{2,3},{3,2},{4,5},{5,4},{6,7},{7,6},{8,9},{9,8},{10,11... | collective-permute-start | bytes 3342344 | tf_op jit(solution)/shard_map/ppermute | solution.py:272
  48.0 11.6 %collective-permute-start.17 = (bf16[256,2176]{1,0:T(8,128)(2,1)S(1)}, bf16[256,2176]{1,0:T(8,128)(2,1)S(1)}, u32[]{:S(2)}, u32[]{:S(2)}) collective-permute-start(bf16[256,2176]{1,0:T(8,128)(2,1)S(1)} %collective-permute-done.16.refs_17_), channel_id=1, source_target_pairs={{0,1},{1,0},{2,3},{3,2},{4,5},{5,4},{6,7},{7,6},{8,9},{9,8},{10,11... | collective-permute-start | bytes 3342344 | tf_op jit(solution)/shard_map/ppermute | solution.py:272
  52.2 13.0 %collective-permute-start = (bf16[64,2176]{1,0:T(8,128)(2,1)S(1)}, bf16[64,2176]{1,0:T(8,128)(2,1)S(1)}, u32[]{:S(2)}, u32[]{:S(2)}) collective-permute-start(bf16[64,2176]{1,0:T(8,128)(2,1)S(1)} %bitcast.16), channel_id=1, source_target_pairs={{0,16},{1,17},{2,18},{3,19},{4,20},{5,21},{6,22},{7,23},{8,24},{9,... | collective-permute-start | bytes 835592 | tf_op jit(solution)/shard_map/ppermute | solution.py:272
  53.3 6.2 %collective-permute-start.13 = (bf16[32,2176]{1,0:T(8,128)(2,1)S(1)}, bf16[32,2176]{1,0:T(8,128)(2,1)S(1)}, u32[]{:S(2)}, u32[]{:S(2)}) collective-permute-start(bf16[32,2176]{1,0:T(8,128)(2,1)S(1)} %collective-permute-done.9.refs_9_), channel_id=1, source_target_pairs={{0,2},{1,3},{2,4},{3,5},{4,6},{5,7},{6,8},{7,9},{8,10},{9,11},{10,... | collective-permute-start | bytes 417800 | tf_op jit(solution)/shard_map/ppermute | solution.py:272
  53.9 5.7 %collective-permute-start.14 = (bf16[32,2176]{1,0:T(8,128)(2,1)S(1)}, bf16[32,2176]{1,0:T(8,128)(2,1)S(1)}, u32[]{:S(2)}, u32[]{:S(2)}) collective-permute-start(bf16[32,2176]{1,0:T(8,128)(2,1)S(1)} %collective-permute-done.12.refs_6_), channel_id=1, source_target_pairs={{0,14},{1,15},{2,0},{3,1},{4,2},{5,3},{6,4},{7,5},{8,6},{9,7},{10,... | collective-permute-start | bytes 417800 | tf_op jit(solution)/shard_map/ppermute | solution.py:272
  59.5 1.3 copy-start
  65.2 8.3 %collective-permute-start.22 = (bf16[64,2176]{1,0:T(8,128)(2,1)S(1)}, bf16[64,2176]{1,0:T(8,128)(2,1)S(1)}, u32[]{:S(2)}, u32[]{:S(2)}) collective-permute-start(bf16[64,2176]{1,0:T(8,128)(2,1)S(1)} %collective-permute-done.refs_0_), channel_id=1, source_target_pairs={{0,2},{1,3},{2,4},{3,5},{4,6},{5,7},{6,8},{7,9},{8,10},{9,11},{10,... | collective-permute-start | bytes 835592 | tf_op jit(solution)/shard_map/ppermute | solution.py:272
  65.2 8.3 %collective-permute-start.19 = (bf16[64,2176]{1,0:T(8,128)(2,1)S(1)}, bf16[64,2176]{1,0:T(8,128)(2,1)S(1)}, u32[]{:S(2)}, u32[]{:S(2)}) collective-permute-start(bf16[64,2176]{1,0:T(8,128)(2,1)S(1)} %collective-permute-done.refs_0_), channel_id=1, source_target_pairs={{0,14},{1,15},{2,0},{3,1},{4,2},{5,3},{6,4},{7,5},{8,6},{9,7},{10,... | collective-permute-start | bytes 835592 | tf_op jit(solution)/shard_map/ppermute | solution.py:272
  67.8 31.2 %all-to-all-start.1 = ((f32[8,64,1024]{2,1,0:T(8,128)}), f32[8,64,1024]{2,1,0:T(8,128)}, u32[]{:S(2)}, u32[]{:S(2)}) async-start(f32[8,64,1024]{2,1,0:T(8,128)} %get-tuple-element.41), calls=%async_computation.1 | async-start | bytes 4194304 | tf_op jit(solution)/shard_map/all_to_all | solution.py:327
  73.4 7.4 %collective-permute-start.23 = (bf16[64,2176]{1,0:T(8,128)(2,1)S(1)}, bf16[64,2176]{1,0:T(8,128)(2,1)S(1)}, u32[]{:S(2)}, u32[]{:S(2)}) collective-permute-start(bf16[64,2176]{1,0:T(8,128)(2,1)S(1)} %collective-permute-done.22.refs_8_), channel_id=1, source_target_pairs={{0,2},{1,3},{2,4},{3,5},{4,6},{5,7},{6,8},{7,9},{8,10},{9,11},{10,... | collective-permute-start | bytes 835592 | tf_op jit(solution)/shard_map/ppermute | solution.py:272
  73.4 7.4 %collective-permute-start.20 = (bf16[64,2176]{1,0:T(8,128)(2,1)S(1)}, bf16[64,2176]{1,0:T(8,128)(2,1)S(1)}, u32[]{:S(2)}, u32[]{:S(2)}) collective-permute-start(bf16[64,2176]{1,0:T(8,128)(2,1)S(1)} %collective-permute-done.19.refs_1_), channel_id=1, source_target_pairs={{0,14},{1,15},{2,0},{3,1},{4,2},{5,3},{6,4},{7,5},{8,6},{9,7},{10,... | collective-permute-start | bytes 835592 | tf_op jit(solution)/shard_map/ppermute | solution.py:272
  80.9 7.0 %collective-permute-start.24 = (bf16[64,2176]{1,0:T(8,128)(2,1)S(1)}, bf16[64,2176]{1,0:T(8,128)(2,1)S(1)}, u32[]{:S(2)}, u32[]{:S(2)}) collective-permute-start(bf16[64,2176]{1,0:T(8,128)(2,1)S(1)} %collective-permute-done.23.refs_7_), channel_id=1, source_target_pairs={{0,2},{1,3},{2,4},{3,5},{4,6},{5,7},{6,8},{7,9},{8,10},{9,11},{10,... | collective-permute-start | bytes 835592 | tf_op jit(solution)/shard_map/ppermute | solution.py:272
  80.9 7.1 %collective-permute-start.21 = (bf16[64,2176]{1,0:T(8,128)(2,1)S(1)}, bf16[64,2176]{1,0:T(8,128)(2,1)S(1)}, u32[]{:S(2)}, u32[]{:S(2)}) collective-permute-start(bf16[64,2176]{1,0:T(8,128)(2,1)S(1)} %collective-permute-done.20.refs_2_), channel_id=1, source_target_pairs={{0,14},{1,15},{2,0},{3,1},{4,2},{5,3},{6,4},{7,5},{8,6},{9,7},{10,... | collective-permute-start | bytes 835592 | tf_op jit(solution)/shard_map/ppermute | solution.py:272
  87.9 7.0 %collective-permute-start.25 = (bf16[32,2176]{1,0:T(8,128)(2,1)S(1)}, bf16[32,2176]{1,0:T(8,128)(2,1)S(1)}, u32[]{:S(2)}, u32[]{:S(2)}) collective-permute-start(bf16[32,2176]{1,0:T(8,128)(2,1)S(1)} %slice.26), channel_id=1, source_target_pairs={{0,2},{1,3},{2,4},{3,5},{4,6},{5,7},{6,8},{7,9},{8,10},{9,11},{10,... | collective-permute-start | bytes 417800 | tf_op jit(solution)/shard_map/ppermute | solution.py:272
  88.0 6.9 %collective-permute-start.26 = (bf16[32,2176]{1,0:T(8,128)(2,1)S(1)}, bf16[32,2176]{1,0:T(8,128)(2,1)S(1)}, u32[]{:S(2)}, u32[]{:S(2)}) collective-permute-start(bf16[32,2176]{1,0:T(8,128)(2,1)S(1)} %slice.27), channel_id=1, source_target_pairs={{0,14},{1,15},{2,0},{3,1},{4,2},{5,3},{6,4},{7,5},{8,6},{9,7},{10,... | collective-permute-start | bytes 417800 | tf_op jit(solution)/shard_map/ppermute | solution.py:272
  90.7 8.3 %copy-start.3 = (s32[3]{0:T(128)S(1)}, s32[3]{0:T(128)}, u32[]{:S(2)}) copy-start(s32[3]{0:T(128)} %pad_add_fusion.place) | copy-start | bytes 40
  90.7 32.9 %collective-permute-start.18 = (bf16[512,2176]{1,0:T(8,128)(2,1)}, bf16[512,2176]{1,0:T(8,128)(2,1)}, u32[]{:S(2)}, u32[]{:S(2)}) collective-permute-start(bf16[512,2176]{1,0:T(8,128)(2,1)} %get-tuple-element.45.refs_0_), channel_id=1, source_target_pairs={{0,1},{1,0},{2,3},{3,2},{4,5},{5,4},{6,7},{7,6},{8,9},{9,8},{10,11... | collective-permute-start | bytes 6684680 | tf_op jit(solution)/shard_map/ppermute | solution.py:272
  95.1 42.6 %collective-permute-start.27 = (bf16[512,2176]{1,0:T(8,128)(2,1)S(1)}, bf16[512,2176]{1,0:T(8,128)(2,1)}, u32[]{:S(2)}, u32[]{:S(2)}) collective-permute-start(bf16[512,2176]{1,0:T(8,128)(2,1)S(1)} %shard_map.91.refs_2_), channel_id=1, source_target_pairs={{0,1},{1,0},{2,3},{3,2},{4,5},{5,4},{6,7},{7,6},{8,9},{9,8},{10,11... | collective-permute-start | bytes 6684680 | tf_op jit(solution)/shard_map/ppermute | solution.py:272
  101.5 9.8 %all-to-all-start.2 = ((f32[8,1,128]{2,1,0:T(1,128)}), f32[8,1,128]{2,1,0:T(1,128)S(1)}, u32[]{:S(2)}, u32[]{:S(2)}) async-start(f32[8,1,128]{2,1,0:T(1,128)} %get-tuple-element.43), calls=%async_computation.2 | async-start | bytes 8192 | tf_op jit(solution)/shard_map/all_to_all | solution.py:355
  112.1 1.0 copy-start.2
  113.1 24.5 %all-to-all-start.3 = ((bf16[32,64,256]{2,1,0:T(8,128)(2,1)}), bf16[32,64,256]{2,1,0:T(8,128)(2,1)S(1)}, u32[]{:S(2)}, u32[]{:S(2)}) async-start(bf16[32,64,256]{2,1,0:T(8,128)(2,1)} %copy-done.2), calls=%async_computation.3 | async-start | bytes 2097152 | tf_op jit(solution)/shard_map/all_to_all | solution.py:367
  120.3 17.3 %copy-start.4 = (s32[3]{0:T(128)S(1)}, s32[3]{0:T(128)}, u32[]{:S(2)}) copy-start(s32[3]{0:T(128)} %pad_add_fusion.place) | copy-start | bytes 40
  120.3 17.3 %copy-start.5 = (f32[256]{0:T(256)S(1)}, f32[256]{0:T(256)}, u32[]{:S(2)}) copy-start(f32[256]{0:T(256)} %param.13) | copy-start | bytes 3076
  137.6 1.0 copy-start.1

commit v3 on v2

--- a/solution.py
+++ b/solution.py
@@ -15,6 +15,7 @@
 VMEM = pl.BlockSpec(memory_space=pltpu.VMEM)
 SMEM = pl.BlockSpec(memory_space=pltpu.SMEM)
 ANY = pl.BlockSpec(memory_space=pl.ANY)
+LESS = pltpu.CompilerParams(vmem_limit_bytes=16 << 20)
 ROOM = pltpu.CompilerParams(vmem_limit_bytes=24 << 20)
 WIDE = pltpu.CompilerParams(vmem_limit_bytes=56 << 20)
 
@@ -299,17 +300,14 @@
     table_x = send("side", lax.optimization_barrier((table, block))[0])
     beside = send("side", block)
 
-    up = [block[:half], block[half:]]
-    down = list(up)
+    up = down = block
     held = {0: [block]}
     for step in range(1, depth // 2):
-        for h in range(2):
-            sent = (send("up", up[h]), send("down", down[h]))
-            up[h], down[h] = lax.optimization_barrier(sent + (up[1 - h], down[1 - h]))[:2]
-        held[depth - step] = list(up)
-        held[step] = list(down)
-    table_x = lax.optimization_barrier((table_x, up[1], down[1]))[0]
-    held[depth // 2] = [send("up", up[0]), send("down", down[1])]
+        up, down = send("up", up), send("down", down)
+        held[depth - step] = [up]
+        held[step] = [down]
+    table_x = lax.optimization_barrier((table_x, up, down))[0]
+    held[depth // 2] = [send("up", up[:half]), send("down", down[half:])]
     tables4 = [table, send("core", table), table_x, send("core", table_x)]
     blocks = [held[o] for o in range(depth)]
     counts = [len(v) for v in blocks]
@@ -350,7 +348,7 @@
         ),
         in_specs=[SMEM, VMEM],
         out_specs=(VMEM, VMEM),
-        compiler_params=ROOM,
+        compiler_params=LESS,
     )(place, parts)
     stats = lax.all_to_all(stats, "ref", 0, 0, tiled=True, axis_index_groups=tables["column"])
     weights, evidence = pl.pallas_call(

time: 146 us -> 146 us (level)
  starting transfers between devices: 69.4 us -> 67.4 us
  waiting for transfers between devices: 43.8 us -> 45.4 us
    ppermute x28 -> x22, starting transfers between devices: 46.8 us -> 42.6 us  [send(): return lax.ppermute(value, axis, pairs)]
    all_to_all x1, starting transfers between devices: 3.53 us -> 5.56 us  [local(): lax.all_to_all(stats, 'ref', 0, 0, tiled=True, axis_index_groups=tables['...]
    ppermute x28 -> x22, waiting for transfers between devices: 21.8 us -> 23.2 us  [send(): return lax.ppermute(value, axis, pairs)]
    unnamed x13 -> x11, local copies, waits for them, and re-layouts: 4.61 us -> 4.58 us
  transfers between devices with their start and end apart: 32 -> 26, of which waited for: 14 -> 10; matrix products, arithmetic and copies ran while one was open for 4% -> 4% of each run, Pallas kernels for 8% -> 8%
where the time goes in v3:
time: 146 us; the launch traced here: 145 us
  starting transfers between devices  67.4 us (46%)
  waiting for transfers between devices  45.4 us (31%)
  Pallas kernels  22 us (15%)
  local copies, waits for them, and re-layouts  6.25 us (4%)
  other arithmetic  3.37 us (2%)
    ppermute x22, starting transfers between devices, send(): return lax.ppermute(value, axis, pairs)  42.6 us
    ppermute x22, waiting for transfers between devices, send(): return lax.ppermute(value, axis, pairs)  23.2 us
    all_to_all x1, waiting for transfers between devices, local(): lax.all_to_all(weights, ('dom', 'ref'), 0, 0, tiled=True, axis_index_grou...  14 us
    all_to_all x1, starting transfers between devices, local(): block = lax.all_to_all(pieces, 'dom', 0, 0, tiled=True)  7.49 us
    all_to_all x1, starting transfers between devices, local(): lax.all_to_all(weights, ('dom', 'ref'), 0, 0, tiled=True, axis_index_grou...  7.32 us
    pallas_call x1, Pallas kernels, local(): pl.pallas_call(renew_kernel, out_shape=jax.ShapeDtypeStruct((share, n_own...  7.12 us
    all_to_all x1, starting transfers between devices, local(): lax.all_to_all(stats, 'ref', 0, 0, tiled=True, axis_index_groups=tables['...  5.56 us
    unnamed x11, local copies, waits for them, and re-layouts  4.58 us
  transfers between devices with their start and end apart: 26, of which 10 were waited for; matrix products, arithmetic and copies ran while one was open for 4% of the time, Pallas kernels for 8%

profile of v3, /device:TPU:1, one launch (start us, length us, event | category | flops | bytes accessed | tf_op | source)
XLA Modules:
  0.0 145.2 jit_solution(13385970554574684471)
XLA Ops:
  0.6 3.3 %shard_map.86 = bf16[8,8,2176]{2,1,0:T(8,128)(2,1)} custom-call(s32[2,8]{1,0:T(2,128)} %bitcast.18, s32[8]{0:T(128)} %groups.1, f32[8]{0:T(128)} %precision.1, bf16[8,16384]{1,0:T(8,128)(2,1)} %particles.1, f32[32,16384]{1,0:T(8,128)} %ctf.3), custom_call_target="tpu_custom_call" | custom-call | tf_op jit(solution)/shard_map/pallas_call | solution.py:77
  3.9 7.5 %all-to-all-start = ((bf16[8,8,2176]{2,1,0:T(8,128)(2,1)}), bf16[8,8,2176]{2,1,0:T(8,128)(2,1)S(1)}, u32[]{:S(2)}, u32[]{:S(2)}) async-start(bf16[8,8,2176]{2,1,0:T(8,128)(2,1)} %shard_map.86), calls=%async_computation | async-start | bytes 557056 | tf_op jit(solution)/shard_map/all_to_all | solution.py:297
  11.4 0.6 pad_add_fusion.place
  12.0 3.9 %shard_map.87.refs_9_ = bf16[256,2176]{1,0:T(8,128)(2,1)} custom-call(s32[3]{0:T(128)} %pad_add_fusion.place, bf16[256,16384]{1,0:T(8,128)(2,1)} %references.1, f32[32,16384]{1,0:T(8,128)} %ctf.3), custom_call_target="tpu_custom_call" | custom-call | flops 536870912 | bytes 8388608 | tf_op jit(solution)/shard_map/pallas_call | solution.py:126
  15.9 3.2 %all-to-all-done = bf16[8,8,2176]{2,1,0:T(8,128)(2,1)S(1)} async-done(((bf16[8,8,2176]{2,1,0:T(8,128)(2,1)}), bf16[8,8,2176]{2,1,0:T(8,128)(2,1)S(1)}, u32[]{:S(2)}, u32[]{:S(2)}) %all-to-all-start) | async-done | bytes 278560 | tf_op jit(solution)/shard_map/all_to_all | solution.py:297
  19.1 0.3 collective-permute-start.10
  19.4 1.6 %collective-permute-start.4 = (bf16[64,2176]{1,0:T(8,128)(2,1)S(1)}, bf16[64,2176]{1,0:T(8,128)(2,1)S(1)}, u32[]{:S(2)}, u32[]{:S(2)}) collective-permute-start(bf16[64,2176]{1,0:T(8,128)(2,1)S(1)} %bitcast.12), channel_id=1, source_target_pairs={{0,2},{1,3},{2,4},{3,5},{4,6},{5,7},{6,8},{7,9},{8,10},{9,11},{10,... | collective-permute-start | bytes 835592 | tf_op jit(solution)/shard_map/ppermute | solution.py:273
  21.1 3.9 %collective-permute-start.1 = (bf16[64,2176]{1,0:T(8,128)(2,1)S(1)}, bf16[64,2176]{1,0:T(8,128)(2,1)S(1)}, u32[]{:S(2)}, u32[]{:S(2)}) collective-permute-start(bf16[64,2176]{1,0:T(8,128)(2,1)S(1)} %bitcast.13), channel_id=1, source_target_pairs={{0,14},{1,15},{2,0},{3,1},{4,2},{5,3},{6,4},{7,5},{8,6},{9,7},{10,... | collective-permute-start | bytes 835592 | tf_op jit(solution)/shard_map/ppermute | solution.py:273
  25.0 4.5 %collective-permute-done.4.refs_8_ = bf16[64,2176]{1,0:T(8,128)(2,1)S(1)} collective-permute-done((bf16[64,2176]{1,0:T(8,128)(2,1)S(1)}, bf16[64,2176]{1,0:T(8,128)(2,1)S(1)}, u32[]{:S(2)}, u32[]{:S(2)}) %collective-permute-start.4) | collective-permute-done | bytes 278560 | tf_op jit(solution)/shard_map/ppermute | solution.py:273
  29.5 0.0 collective-permute-start.5
  29.5 0.0 collective-permute-done.1.refs_1_
  29.6 2.7 %collective-permute-start.2 = (bf16[64,2176]{1,0:T(8,128)(2,1)S(1)}, bf16[64,2176]{1,0:T(8,128)(2,1)S(1)}, u32[]{:S(2)}, u32[]{:S(2)}) collective-permute-start(bf16[64,2176]{1,0:T(8,128)(2,1)S(1)} %collective-permute-done.1.refs_1_), channel_id=1, source_target_pairs={{0,14},{1,15},{2,0},{3,1},{4,2},{5,3},{6,4},{7,5},{8,6},{9,7},{10,... | collective-permute-start | bytes 835592 | tf_op jit(solution)/shard_map/ppermute | solution.py:273
  32.2 3.9 %collective-permute-done.5.refs_7_ = bf16[64,2176]{1,0:T(8,128)(2,1)S(1)} collective-permute-done((bf16[64,2176]{1,0:T(8,128)(2,1)S(1)}, bf16[64,2176]{1,0:T(8,128)(2,1)S(1)}, u32[]{:S(2)}, u32[]{:S(2)}) %collective-permute-start.5) | collective-permute-done | bytes 278560 | tf_op jit(solution)/shard_map/ppermute | solution.py:273
  36.2 0.0 collective-permute-start.6
  36.2 0.0 collective-permute-done.2.refs_2_
  36.2 2.7 %collective-permute-start.3 = (bf16[64,2176]{1,0:T(8,128)(2,1)S(1)}, bf16[64,2176]{1,0:T(8,128)(2,1)S(1)}, u32[]{:S(2)}, u32[]{:S(2)}) collective-permute-start(bf16[64,2176]{1,0:T(8,128)(2,1)S(1)} %collective-permute-done.2.refs_2_), channel_id=1, source_target_pairs={{0,14},{1,15},{2,0},{3,1},{4,2},{5,3},{6,4},{7,5},{8,6},{9,7},{10,... | collective-permute-start | bytes 835592 | tf_op jit(solution)/shard_map/ppermute | solution.py:273
  38.8 4.9 %collective-permute-start.9 = (bf16[256,2176]{1,0:T(8,128)(2,1)}, bf16[256,2176]{1,0:T(8,128)(2,1)S(1)}, u32[]{:S(2)}, u32[]{:S(2)}) collective-permute-start(bf16[256,2176]{1,0:T(8,128)(2,1)} %shard_map.87.refs_9_), channel_id=1, source_target_pairs={{0,1},{1,0},{2,3},{3,2},{4,5},{5,4},{6,7},{7,6},{8,9},{9,8},{10,11... | collective-permute-start | bytes 3342344 | tf_op jit(solution)/shard_map/ppermute | solution.py:273
  43.8 0.0 collective-permute-done.6.refs_6_
  43.8 4.4 %collective-permute-start.11 = (bf16[256,2176]{1,0:T(8,128)(2,1)S(1)}, bf16[256,2176]{1,0:T(8,128)(2,1)S(1)}, u32[]{:S(2)}, u32[]{:S(2)}) collective-permute-start(bf16[256,2176]{1,0:T(8,128)(2,1)S(1)} %collective-permute-done.10.refs_11_), channel_id=1, source_target_pairs={{0,1},{1,0},{2,3},{3,2},{4,5},{5,4},{6,7},{7,6},{8,9},{9,8},{10,11... | collective-permute-start | bytes 3342344 | tf_op jit(solution)/shard_map/ppermute | solution.py:273
  48.2 1.2 collective-permute-start
  49.3 0.1 collective-permute-start.7
  49.4 3.1 %collective-permute-start.8 = (bf16[32,2176]{1,0:T(8,128)(2,1)S(1)}, bf16[32,2176]{1,0:T(8,128)(2,1)S(1)}, u32[]{:S(2)}, u32[]{:S(2)}) collective-permute-start(bf16[32,2176]{1,0:T(8,128)(2,1)S(1)} %slice.17), channel_id=1, source_target_pairs={{0,14},{1,15},{2,0},{3,1},{4,2},{5,3},{6,4},{7,5},{8,6},{9,7},{10,... | collective-permute-start | bytes 417800 | tf_op jit(solution)/shard_map/ppermute | solution.py:273
  52.6 0.0 collective-permute-done.9.refs_10_
  52.6 3.7 %collective-permute-done.7.refs_4_ = bf16[32,2176]{1,0:T(8,128)(2,1)S(1)} collective-permute-done((bf16[32,2176]{1,0:T(8,128)(2,1)S(1)}, bf16[32,2176]{1,0:T(8,128)(2,1)S(1)}, u32[]{:S(2)}, u32[]{:S(2)}) %collective-permute-start.7) | collective-permute-done | bytes 139296 | tf_op jit(solution)/shard_map/ppermute | solution.py:273
  56.3 1.2 copy-done
  57.6 4.3 %shard_map.88 = (f32[8,64,1024]{2,1,0:T(8,128)}, bf16[512,2176]{1,0:T(8,128)(2,1)}) custom-call(bf16[64,2176]{1,0:T(8,128)(2,1)S(1)} %bitcast.15, bf16[64,2176]{1,0:T(8,128)(2,1)S(1)} %collective-permute-done.1.refs_1_, bf16[64,2176]{1,0:T(8,128)(2,1)S(1)} %collective-permute-done.2.refs_2_, bf16[64,2176]{1,0:T(8,128)(2,1)S(1)} %collective-permute-done.3.refs_3_, ...), custom_call_target="tpu_custom_call" | custom-call | tf_op jit(solution)/shard_map/pallas_call | solution.py:314
  61.9 0.0 collective-permute-done.refs_0_
  61.9 2.2 %collective-permute-start.16 = (bf16[64,2176]{1,0:T(8,128)(2,1)S(1)}, bf16[64,2176]{1,0:T(8,128)(2,1)S(1)}, u32[]{:S(2)}, u32[]{:S(2)}) collective-permute-start(bf16[64,2176]{1,0:T(8,128)(2,1)S(1)} %collective-permute-done.refs_0_), channel_id=1, source_target_pairs={{0,2},{1,3},{2,4},{3,5},{4,6},{5,7},{6,8},{7,9},{8,10},{9,11},{10,... | collective-permute-start | bytes 835592 | tf_op jit(solution)/shard_map/ppermute | solution.py:273
  64.2 0.4 collective-permute-start.13
  64.6 4.4 %all-to-all-start.1 = ((f32[8,64,1024]{2,1,0:T(8,128)}), f32[8,64,1024]{2,1,0:T(8,128)}, u32[]{:S(2)}, u32[]{:S(2)}) async-start(f32[8,64,1024]{2,1,0:T(8,128)} %get-tuple-element.17), calls=%async_computation.1 | async-start | bytes 4194304 | tf_op jit(solution)/shard_map/all_to_all | solution.py:325
  69.0 1.6 %collective-permute-done.16.refs_8_ = bf16[64,2176]{1,0:T(8,128)(2,1)S(1)} collective-permute-done((bf16[64,2176]{1,0:T(8,128)(2,1)S(1)}, bf16[64,2176]{1,0:T(8,128)(2,1)S(1)}, u32[]{:S(2)}, u32[]{:S(2)}) %collective-permute-start.16) | collective-permute-done | bytes 278560 | tf_op jit(solution)/shard_map/ppermute | solution.py:273
  70.6 0.7 collective-permute-start.17
  71.2 0.0 collective-permute-done.13.refs_1_
  71.2 2.0 %collective-permute-start.14 = (bf16[64,2176]{1,0:T(8,128)(2,1)S(1)}, bf16[64,2176]{1,0:T(8,128)(2,1)S(1)}, u32[]{:S(2)}, u32[]{:S(2)}) collective-permute-start(bf16[64,2176]{1,0:T(8,128)(2,1)S(1)} %collective-permute-done.13.refs_1_), channel_id=1, source_target_pairs={{0,14},{1,15},{2,0},{3,1},{4,2},{5,3},{6,4},{7,5},{8,6},{9,7},{10,... | collective-permute-start | bytes 835592 | tf_op jit(solution)/shard_map/ppermute | solution.py:273
  73.2 5.1 %collective-permute-done.17.refs_7_ = bf16[64,2176]{1,0:T(8,128)(2,1)S(1)} collective-permute-done((bf16[64,2176]{1,0:T(8,128)(2,1)S(1)}, bf16[64,2176]{1,0:T(8,128)(2,1)S(1)}, u32[]{:S(2)}, u32[]{:S(2)}) %collective-permute-start.17) | collective-permute-done | bytes 278560 | tf_op jit(solution)/shard_map/ppermute | solution.py:273
  78.3 0.0 collective-permute-done.14.refs_2_
  78.4 2.7 %collective-permute-start.15 = (bf16[64,2176]{1,0:T(8,128)(2,1)S(1)}, bf16[64,2176]{1,0:T(8,128)(2,1)S(1)}, u32[]{:S(2)}, u32[]{:S(2)}) collective-permute-start(bf16[64,2176]{1,0:T(8,128)(2,1)S(1)} %collective-permute-done.14.refs_2_), channel_id=1, source_target_pairs={{0,14},{1,15},{2,0},{3,1},{4,2},{5,3},{6,4},{7,5},{8,6},{9,7},{10,... | collective-permute-start | bytes 835592 | tf_op jit(solution)/shard_map/ppermute | solution.py:273
  81.0 4.3 %collective-permute-done.18.refs_6_ = bf16[64,2176]{1,0:T(8,128)(2,1)S(1)} collective-permute-done((bf16[64,2176]{1,0:T(8,128)(2,1)S(1)}, bf16[64,2176]{1,0:T(8,128)(2,1)S(1)}, u32[]{:S(2)}, u32[]{:S(2)}) %collective-permute-start.18) | collective-permute-done | bytes 278560 | tf_op jit(solution)/shard_map/ppermute | solution.py:273
  85.4 0.1 collective-permute-start.19
  85.5 2.7 %collective-permute-start.20 = (bf16[32,2176]{1,0:T(8,128)(2,1)S(1)}, bf16[32,2176]{1,0:T(8,128)(2,1)S(1)}, u32[]{:S(2)}, u32[]{:S(2)}) collective-permute-start(bf16[32,2176]{1,0:T(8,128)(2,1)S(1)} %slice.19), channel_id=1, source_target_pairs={{0,14},{1,15},{2,0},{3,1},{4,2},{5,3},{6,4},{7,5},{8,6},{9,7},{10,... | collective-permute-start | bytes 417800 | tf_op jit(solution)/shard_map/ppermute | solution.py:273
  88.2 3.8 %collective-permute-start.12 = (bf16[512,2176]{1,0:T(8,128)(2,1)}, bf16[512,2176]{1,0:T(8,128)(2,1)}, u32[]{:S(2)}, u32[]{:S(2)}) collective-permute-start(bf16[512,2176]{1,0:T(8,128)(2,1)} %get-tuple-element.21.refs_0_), channel_id=1, source_target_pairs={{0,1},{1,0},{2,3},{3,2},{4,5},{5,4},{6,7},{7,6},{8,9},{9,8},{10,11... | collective-permute-start | bytes 6684680 | tf_op jit(solution)/shard_map/ppermute | solution.py:273
  92.1 0.0 collective-permute-done.19.refs_4_
  92.1 0.0 collective-permute-done.20.refs_5_
  92.1 0.2 shard_map.91.refs_2_
  92.2 3.0 %collective-permute-start.21 = (bf16[512,2176]{1,0:T(8,128)(2,1)S(1)}, bf16[512,2176]{1,0:T(8,128)(2,1)}, u32[]{:S(2)}, u32[]{:S(2)}) collective-permute-start(bf16[512,2176]{1,0:T(8,128)(2,1)S(1)} %shard_map.91.refs_2_), channel_id=1, source_target_pairs={{0,1},{1,0},{2,3},{3,2},{4,5},{5,4},{6,7},{7,6},{8,9},{9,8},{10,11... | collective-permute-start | bytes 6684680 | tf_op jit(solution)/shard_map/ppermute | solution.py:273
  95.2 0.9 all-to-all-done.1.parts
  96.1 2.5 %shard_map.89 = (f32[64,1024]{1,0:T(8,128)S(1)}, f32[8,1,128]{2,1,0:T(1,128)}) custom-call(s32[3]{0:T(128)S(1)} %copy-done.3, f32[8,64,1024]{2,1,0:T(8,128)} %all-to-all-done.1.parts), custom_call_target="tpu_custom_call" | custom-call | tf_op jit(solution)/shard_map/pallas_call | solution.py:343
  98.6 5.6 %all-to-all-start.2 = ((f32[8,1,128]{2,1,0:T(1,128)}), f32[8,1,128]{2,1,0:T(1,128)S(1)}, u32[]{:S(2)}, u32[]{:S(2)}) async-start(f32[8,1,128]{2,1,0:T(1,128)} %get-tuple-element.19), calls=%async_computation.2 | async-start | bytes 8192 | tf_op jit(solution)/shard_map/all_to_all | solution.py:353
  104.2 1.0 constant_dynamic-slice_fusion
  105.1 1.3 copy.13
  106.5 0.1 pad.3.clone
  106.5 4.1 %all-to-all-done.2 = f32[8,1,128]{2,1,0:T(1,128)S(1)} async-done(((f32[8,1,128]{2,1,0:T(1,128)}), f32[8,1,128]{2,1,0:T(1,128)S(1)}, u32[]{:S(2)}, u32[]{:S(2)}) %all-to-all-start.2) | async-done | bytes 4128 | tf_op jit(solution)/shard_map/all_to_all | solution.py:353
  110.6 0.8 shard_map.90
  111.4 0.0 copy-start.2
  111.4 1.0 copy-done.2
  112.4 7.3 %all-to-all-start.3 = ((bf16[32,64,256]{2,1,0:T(8,128)(2,1)}), bf16[32,64,256]{2,1,0:T(8,128)(2,1)S(1)}, u32[]{:S(2)}, u32[]{:S(2)}) async-start(bf16[32,64,256]{2,1,0:T(8,128)(2,1)} %copy-done.2), calls=%async_computation.3 | async-start | bytes 2097152 | tf_op jit(solution)/shard_map/all_to_all | solution.py:365
  119.7 0.0 copy-start.4
  119.7 1.4 fusion
  121.2 1.3 maximum_maximum_fusion.square
  122.5 0.6 dynamic-slice_bitcast_fusion
  123.1 14.0 %all-to-all-done.3.spread = bf16[32,64,256]{2,1,0:T(8,128)(2,1)S(1)} async-done(((bf16[32,64,256]{2,1,0:T(8,128)(2,1)}), bf16[32,64,256]{2,1,0:T(8,128)(2,1)S(1)}, u32[]{:S(2)}, u32[]{:S(2)}) %all-to-all-start.3) | async-done | bytes 1048608 | tf_op jit(solution)/shard_map/all_to_all | solution.py:365
  137.0 0.0 collective-permute-done.21.refs_3_
  137.0 1.0 copy-done.1
  138.1 7.1 %shard_map.92 = f32[2048,256]{1,0:T(8,128)} custom-call(s32[3]{0:T(128)S(1)} %copy-done.3, bf16[32,64,256]{2,1,0:T(8,128)(2,1)S(1)} %all-to-all-done.3.spread, bf16[2048,128]{1,0:T(8,128)(2,1)S(1)} %copy-done.1, f32[1,256]{1,0:T(1,128)S(1)} %bitcast.17, bf16[512,2176]{1,0:T(8,128)(2,1)} %get-tuple-element.21.refs_0_, ...), custom_call_target="tpu_custom_call" | custom-call | tf_op jit(solution)/shard_map/pallas_call | solution.py:369
  (17 shorter events, 0.1 us)
Async XLA Ops:
  3.9 15.2 %all-to-all-start = ((bf16[8,8,2176]{2,1,0:T(8,128)(2,1)}), bf16[8,8,2176]{2,1,0:T(8,128)(2,1)S(1)}, u32[]{:S(2)}, u32[]{:S(2)}) async-start(bf16[8,8,2176]{2,1,0:T(8,128)(2,1)} %shard_map.86), calls=%async_computation | async-start | bytes 557056 | tf_op jit(solution)/shard_map/all_to_all | solution.py:297
  19.1 24.6 %collective-permute-start.10 = (bf16[256,2176]{1,0:T(8,128)(2,1)}, bf16[256,2176]{1,0:T(8,128)(2,1)S(1)}, u32[]{:S(2)}, u32[]{:S(2)}) collective-permute-start(bf16[256,2176]{1,0:T(8,128)(2,1)} %shard_map.87.refs_9_), channel_id=1, source_target_pairs={{0,16},{1,17},{2,18},{3,19},{4,20},{5,21},{6,22},{7,23},{8,24},{9,... | collective-permute-start | bytes 3342344 | tf_op jit(solution)/shard_map/ppermute | solution.py:273
  19.4 10.1 %collective-permute-start.4 = (bf16[64,2176]{1,0:T(8,128)(2,1)S(1)}, bf16[64,2176]{1,0:T(8,128)(2,1)S(1)}, u32[]{:S(2)}, u32[]{:S(2)}) collective-permute-start(bf16[64,2176]{1,0:T(8,128)(2,1)S(1)} %bitcast.12), channel_id=1, source_target_pairs={{0,2},{1,3},{2,4},{3,5},{4,6},{5,7},{6,8},{7,9},{8,10},{9,11},{10,... | collective-permute-start | bytes 835592 | tf_op jit(solution)/shard_map/ppermute | solution.py:273
  21.1 8.5 %collective-permute-start.1 = (bf16[64,2176]{1,0:T(8,128)(2,1)S(1)}, bf16[64,2176]{1,0:T(8,128)(2,1)S(1)}, u32[]{:S(2)}, u32[]{:S(2)}) collective-permute-start(bf16[64,2176]{1,0:T(8,128)(2,1)S(1)} %bitcast.13), channel_id=1, source_target_pairs={{0,14},{1,15},{2,0},{3,1},{4,2},{5,3},{6,4},{7,5},{8,6},{9,7},{10,... | collective-permute-start | bytes 835592 | tf_op jit(solution)/shard_map/ppermute | solution.py:273
  29.5 6.6 %collective-permute-start.5 = (bf16[64,2176]{1,0:T(8,128)(2,1)S(1)}, bf16[64,2176]{1,0:T(8,128)(2,1)S(1)}, u32[]{:S(2)}, u32[]{:S(2)}) collective-permute-start(bf16[64,2176]{1,0:T(8,128)(2,1)S(1)} %collective-permute-done.4.refs_8_), channel_id=1, source_target_pairs={{0,2},{1,3},{2,4},{3,5},{4,6},{5,7},{6,8},{7,9},{8,10},{9,11},{10,... | collective-permute-start | bytes 835592 | tf_op jit(solution)/shard_map/ppermute | solution.py:273
  29.6 6.6 %collective-permute-start.2 = (bf16[64,2176]{1,0:T(8,128)(2,1)S(1)}, bf16[64,2176]{1,0:T(8,128)(2,1)S(1)}, u32[]{:S(2)}, u32[]{:S(2)}) collective-permute-start(bf16[64,2176]{1,0:T(8,128)(2,1)S(1)} %collective-permute-done.1.refs_1_), channel_id=1, source_target_pairs={{0,14},{1,15},{2,0},{3,1},{4,2},{5,3},{6,4},{7,5},{8,6},{9,7},{10,... | collective-permute-start | bytes 835592 | tf_op jit(solution)/shard_map/ppermute | solution.py:273
  36.2 7.6 %collective-permute-start.6 = (bf16[64,2176]{1,0:T(8,128)(2,1)S(1)}, bf16[64,2176]{1,0:T(8,128)(2,1)S(1)}, u32[]{:S(2)}, u32[]{:S(2)}) collective-permute-start(bf16[64,2176]{1,0:T(8,128)(2,1)S(1)} %collective-permute-done.5.refs_7_), channel_id=1, source_target_pairs={{0,2},{1,3},{2,4},{3,5},{4,6},{5,7},{6,8},{7,9},{8,10},{9,11},{10,... | collective-permute-start | bytes 835592 | tf_op jit(solution)/shard_map/ppermute | solution.py:273
  36.2 7.6 %collective-permute-start.3 = (bf16[64,2176]{1,0:T(8,128)(2,1)S(1)}, bf16[64,2176]{1,0:T(8,128)(2,1)S(1)}, u32[]{:S(2)}, u32[]{:S(2)}) collective-permute-start(bf16[64,2176]{1,0:T(8,128)(2,1)S(1)} %collective-permute-done.2.refs_2_), channel_id=1, source_target_pairs={{0,14},{1,15},{2,0},{3,1},{4,2},{5,3},{6,4},{7,5},{8,6},{9,7},{10,... | collective-permute-start | bytes 835592 | tf_op jit(solution)/shard_map/ppermute | solution.py:273
  38.8 13.8 %collective-permute-start.9 = (bf16[256,2176]{1,0:T(8,128)(2,1)}, bf16[256,2176]{1,0:T(8,128)(2,1)S(1)}, u32[]{:S(2)}, u32[]{:S(2)}) collective-permute-start(bf16[256,2176]{1,0:T(8,128)(2,1)} %shard_map.87.refs_9_), channel_id=1, source_target_pairs={{0,1},{1,0},{2,3},{3,2},{4,5},{5,4},{6,7},{7,6},{8,9},{9,8},{10,11... | collective-permute-start | bytes 3342344 | tf_op jit(solution)/shard_map/ppermute | solution.py:273
  43.8 12.6 %collective-permute-start.11 = (bf16[256,2176]{1,0:T(8,128)(2,1)S(1)}, bf16[256,2176]{1,0:T(8,128)(2,1)S(1)}, u32[]{:S(2)}, u32[]{:S(2)}) collective-permute-start(bf16[256,2176]{1,0:T(8,128)(2,1)S(1)} %collective-permute-done.10.refs_11_), channel_id=1, source_target_pairs={{0,1},{1,0},{2,3},{3,2},{4,5},{5,4},{6,7},{7,6},{8,9},{9,8},{10,11... | collective-permute-start | bytes 3342344 | tf_op jit(solution)/shard_map/ppermute | solution.py:273
  48.2 13.8 %collective-permute-start = (bf16[64,2176]{1,0:T(8,128)(2,1)S(1)}, bf16[64,2176]{1,0:T(8,128)(2,1)S(1)}, u32[]{:S(2)}, u32[]{:S(2)}) collective-permute-start(bf16[64,2176]{1,0:T(8,128)(2,1)S(1)} %bitcast.14), channel_id=1, source_target_pairs={{0,16},{1,17},{2,18},{3,19},{4,20},{5,21},{6,22},{7,23},{8,24},{9,... | collective-permute-start | bytes 835592 | tf_op jit(solution)/shard_map/ppermute | solution.py:273
  49.3 7.0 %collective-permute-start.7 = (bf16[32,2176]{1,0:T(8,128)(2,1)S(1)}, bf16[32,2176]{1,0:T(8,128)(2,1)S(1)}, u32[]{:S(2)}, u32[]{:S(2)}) collective-permute-start(bf16[32,2176]{1,0:T(8,128)(2,1)S(1)} %slice.16), channel_id=1, source_target_pairs={{0,2},{1,3},{2,4},{3,5},{4,6},{5,7},{6,8},{7,9},{8,10},{9,11},{10,... | collective-permute-start | bytes 417800 | tf_op jit(solution)/shard_map/ppermute | solution.py:273
  49.4 6.9 %collective-permute-start.8 = (bf16[32,2176]{1,0:T(8,128)(2,1)S(1)}, bf16[32,2176]{1,0:T(8,128)(2,1)S(1)}, u32[]{:S(2)}, u32[]{:S(2)}) collective-permute-start(bf16[32,2176]{1,0:T(8,128)(2,1)S(1)} %slice.17), channel_id=1, source_target_pairs={{0,14},{1,15},{2,0},{3,1},{4,2},{5,3},{6,4},{7,5},{8,6},{9,7},{10,... | collective-permute-start | bytes 417800 | tf_op jit(solution)/shard_map/ppermute | solution.py:273
  56.3 1.2 copy-start
  61.9 8.6 %collective-permute-start.16 = (bf16[64,2176]{1,0:T(8,128)(2,1)S(1)}, bf16[64,2176]{1,0:T(8,128)(2,1)S(1)}, u32[]{:S(2)}, u32[]{:S(2)}) collective-permute-start(bf16[64,2176]{1,0:T(8,128)(2,1)S(1)} %collective-permute-done.refs_0_), channel_id=1, source_target_pairs={{0,2},{1,3},{2,4},{3,5},{4,6},{5,7},{6,8},{7,9},{8,10},{9,11},{10,... | collective-permute-start | bytes 835592 | tf_op jit(solution)/shard_map/ppermute | solution.py:273
  64.2 7.1 %collective-permute-start.13 = (bf16[64,2176]{1,0:T(8,128)(2,1)S(1)}, bf16[64,2176]{1,0:T(8,128)(2,1)S(1)}, u32[]{:S(2)}, u32[]{:S(2)}) collective-permute-start(bf16[64,2176]{1,0:T(8,128)(2,1)S(1)} %collective-permute-done.refs_0_), channel_id=1, source_target_pairs={{0,14},{1,15},{2,0},{3,1},{4,2},{5,3},{6,4},{7,5},{8,6},{9,7},{10,... | collective-permute-start | bytes 835592 | tf_op jit(solution)/shard_map/ppermute | solution.py:273
  64.6 31.5 %all-to-all-start.1 = ((f32[8,64,1024]{2,1,0:T(8,128)}), f32[8,64,1024]{2,1,0:T(8,128)}, u32[]{:S(2)}, u32[]{:S(2)}) async-start(f32[8,64,1024]{2,1,0:T(8,128)} %get-tuple-element.17), calls=%async_computation.1 | async-start | bytes 4194304 | tf_op jit(solution)/shard_map/all_to_all | solution.py:325
  70.6 7.8 %collective-permute-start.17 = (bf16[64,2176]{1,0:T(8,128)(2,1)S(1)}, bf16[64,2176]{1,0:T(8,128)(2,1)S(1)}, u32[]{:S(2)}, u32[]{:S(2)}) collective-permute-start(bf16[64,2176]{1,0:T(8,128)(2,1)S(1)} %collective-permute-done.16.refs_8_), channel_id=1, source_target_pairs={{0,2},{1,3},{2,4},{3,5},{4,6},{5,7},{6,8},{7,9},{8,10},{9,11},{10,... | collective-permute-start | bytes 835592 | tf_op jit(solution)/shard_map/ppermute | solution.py:273
  71.2 7.1 %collective-permute-start.14 = (bf16[64,2176]{1,0:T(8,128)(2,1)S(1)}, bf16[64,2176]{1,0:T(8,128)(2,1)S(1)}, u32[]{:S(2)}, u32[]{:S(2)}) collective-permute-start(bf16[64,2176]{1,0:T(8,128)(2,1)S(1)} %collective-permute-done.13.refs_1_), channel_id=1, source_target_pairs={{0,14},{1,15},{2,0},{3,1},{4,2},{5,3},{6,4},{7,5},{8,6},{9,7},{10,... | collective-permute-start | bytes 835592 | tf_op jit(solution)/shard_map/ppermute | solution.py:273
  78.3 7.0 %collective-permute-start.18 = (bf16[64,2176]{1,0:T(8,128)(2,1)S(1)}, bf16[64,2176]{1,0:T(8,128)(2,1)S(1)}, u32[]{:S(2)}, u32[]{:S(2)}) collective-permute-start(bf16[64,2176]{1,0:T(8,128)(2,1)S(1)} %collective-permute-done.17.refs_7_), channel_id=1, source_target_pairs={{0,2},{1,3},{2,4},{3,5},{4,6},{5,7},{6,8},{7,9},{8,10},{9,11},{10,... | collective-permute-start | bytes 835592 | tf_op jit(solution)/shard_map/ppermute | solution.py:273
  78.4 7.1 %collective-permute-start.15 = (bf16[64,2176]{1,0:T(8,128)(2,1)S(1)}, bf16[64,2176]{1,0:T(8,128)(2,1)S(1)}, u32[]{:S(2)}, u32[]{:S(2)}) collective-permute-start(bf16[64,2176]{1,0:T(8,128)(2,1)S(1)} %collective-permute-done.14.refs_2_), channel_id=1, source_target_pairs={{0,14},{1,15},{2,0},{3,1},{4,2},{5,3},{6,4},{7,5},{8,6},{9,7},{10,... | collective-permute-start | bytes 835592 | tf_op jit(solution)/shard_map/ppermute | solution.py:273
  85.4 6.7 %collective-permute-start.19 = (bf16[32,2176]{1,0:T(8,128)(2,1)S(1)}, bf16[32,2176]{1,0:T(8,128)(2,1)S(1)}, u32[]{:S(2)}, u32[]{:S(2)}) collective-permute-start(bf16[32,2176]{1,0:T(8,128)(2,1)S(1)} %slice.18), channel_id=1, source_target_pairs={{0,2},{1,3},{2,4},{3,5},{4,6},{5,7},{6,8},{7,9},{8,10},{9,11},{10,... | collective-permute-start | bytes 417800 | tf_op jit(solution)/shard_map/ppermute | solution.py:273
  85.5 6.6 %collective-permute-start.20 = (bf16[32,2176]{1,0:T(8,128)(2,1)S(1)}, bf16[32,2176]{1,0:T(8,128)(2,1)S(1)}, u32[]{:S(2)}, u32[]{:S(2)}) collective-permute-start(bf16[32,2176]{1,0:T(8,128)(2,1)S(1)} %slice.19), channel_id=1, source_target_pairs={{0,14},{1,15},{2,0},{3,1},{4,2},{5,3},{6,4},{7,5},{8,6},{9,7},{10,... | collective-permute-start | bytes 417800 | tf_op jit(solution)/shard_map/ppermute | solution.py:273
  88.2 7.9 %copy-start.3 = (s32[3]{0:T(128)S(1)}, s32[3]{0:T(128)}, u32[]{:S(2)}) copy-start(s32[3]{0:T(128)} %pad_add_fusion.place) | copy-start | bytes 40
  88.2 34.8 %collective-permute-start.12 = (bf16[512,2176]{1,0:T(8,128)(2,1)}, bf16[512,2176]{1,0:T(8,128)(2,1)}, u32[]{:S(2)}, u32[]{:S(2)}) collective-permute-start(bf16[512,2176]{1,0:T(8,128)(2,1)} %get-tuple-element.21.refs_0_), channel_id=1, source_target_pairs={{0,1},{1,0},{2,3},{3,2},{4,5},{5,4},{6,7},{7,6},{8,9},{9,8},{10,11... | collective-permute-start | bytes 6684680 | tf_op jit(solution)/shard_map/ppermute | solution.py:273
  92.2 44.8 %collective-permute-start.21 = (bf16[512,2176]{1,0:T(8,128)(2,1)S(1)}, bf16[512,2176]{1,0:T(8,128)(2,1)}, u32[]{:S(2)}, u32[]{:S(2)}) collective-permute-start(bf16[512,2176]{1,0:T(8,128)(2,1)S(1)} %shard_map.91.refs_2_), channel_id=1, source_target_pairs={{0,1},{1,0},{2,3},{3,2},{4,5},{5,4},{6,7},{7,6},{8,9},{9,8},{10,11... | collective-permute-start | bytes 6684680 | tf_op jit(solution)/shard_map/ppermute | solution.py:273
  98.6 12.0 %all-to-all-start.2 = ((f32[8,1,128]{2,1,0:T(1,128)}), f32[8,1,128]{2,1,0:T(1,128)S(1)}, u32[]{:S(2)}, u32[]{:S(2)}) async-start(f32[8,1,128]{2,1,0:T(1,128)} %get-tuple-element.19), calls=%async_computation.2 | async-start | bytes 8192 | tf_op jit(solution)/shard_map/all_to_all | solution.py:353
  111.4 1.0 copy-start.2
  112.4 24.6 %all-to-all-start.3 = ((bf16[32,64,256]{2,1,0:T(8,128)(2,1)}), bf16[32,64,256]{2,1,0:T(8,128)(2,1)S(1)}, u32[]{:S(2)}, u32[]{:S(2)}) async-start(bf16[32,64,256]{2,1,0:T(8,128)(2,1)} %copy-done.2), calls=%async_computation.3 | async-start | bytes 2097152 | tf_op jit(solution)/shard_map/all_to_all | solution.py:365
  119.7 17.3 %copy-start.4 = (f32[256]{0:T(256)S(1)}, f32[256]{0:T(256)}, u32[]{:S(2)}) copy-start(f32[256]{0:T(256)} %param.13) | copy-start | bytes 3076
  137.0 1.0 copy-start.1

commit v4 on v3

--- a/solution.py
+++ b/solution.py
@@ -209,25 +209,27 @@
             spread[d * 4 + (q ^ x_c)] = part
 
 
-def renew_kernel(place, spread, square, regularizer, *refs):
+def renew_kernel(orders, place, spread, square, regularizer, *refs):
     lines, (out, table, weights) = refs[:-3], refs[-3:]
     x_c = place[0]
     n_dom, rows, width = spread.shape[0] // 4, spread.shape[1], spread.shape[2]
-    own = 8
+    own = rows // len(orders[0])
     for q in range(4):
         for d in range(n_dom):
             value = spread[d * 4 + (q ^ x_c)].astype(jnp.float32)
-            for o in range(rows // own):
-                at = (o * n_dom + d) * own
+            for k, o in enumerate(orders[q]):
+                at = (k * n_dom + d) * own
                 table[at : at + own, :] = value[o * own : (o + 1) * own, :]
         weights[q * n_dom * rows : (q + 1) * n_dom * rows, :] = table[...].astype(jnp.bfloat16)
 
     def product(first, span):
-        total = jnp.zeros((span, width), jnp.float32)
-        at = 0
+        total, at = 0.0, 0
         for some in lines:
             total = total + lax.dot_general(
-                some[:, first : first + span], weights[at : at + some.shape[0], :], (((0,), (0,)), ((), ())), preferred_element_type=jnp.float32
+                some[:, first : first + span],
+                weights[at : at + some.shape[0], :],
+                (((0,), (0,)), ((), ())),
+                preferred_element_type=jnp.float32,
             )
             at += some.shape[0]
         return total
@@ -324,22 +326,26 @@
     beside, parts = lax.optimization_barrier((beside, parts))
     parts = lax.all_to_all(parts, "dom", 0, 0, tiled=True)
 
+    reach = depth // 4
     up = down = beside
-    found = {0: [beside]}
-    for step in range(1, depth // 2):
+    found = {0: beside}
+    for step in range(1, reach + 1):
         up, down = send("up", up), send("down", down)
-        found[depth - step] = [up]
-        found[step] = [down]
-    found[depth // 2] = [send("up", up[:half]), send("down", down[half:])]
-    found = [v for o in range(depth) for v in found[o]]
+        found[depth - step] = up
+        found[step] = down
+    near = sorted(found)
+    far = [o for o in range(depth) if o not in found]
+    lowest, own_rows = far[0] * n_dom * own, len(far) * n_dom * own
+    found = [found[o] for o in near]
     beside = pl.pallas_call(
         join_kernel,
-        out_shape=jax.ShapeDtypeStruct((n_dom * rows, share + EXTRA), beside.dtype),
+        out_shape=jax.ShapeDtypeStruct((sum(v.shape[0] for v in found), share + EXTRA), mine.dtype),
         in_specs=[VMEM] * len(found),
         out_specs=VMEM,
         compiler_params=ROOM,
     )(*found)
 
+    parts, beside = lax.optimization_barrier((parts, beside))
     score, stats = pl.pallas_call(
         soften_kernel,
         out_shape=(
@@ -350,6 +356,9 @@
         out_specs=(VMEM, VMEM),
         compiler_params=LESS,
     )(place, parts)
+    distant = lax.slice_in_dim(mine, lowest, lowest + own_rows)
+    distant, score = lax.optimization_barrier((distant, score))
+    distant = send("side", distant)
     stats = lax.all_to_all(stats, "ref", 0, 0, tiled=True, axis_index_groups=tables["column"])
     weights, evidence = pl.pallas_call(
         weigh_kernel,
@@ -365,9 +374,10 @@
     weights = lax.all_to_all(
         weights, ("dom", "ref"), 0, 0, tiled=True, axis_index_groups=tables["same_z"]
     )
-    lines = [mine, send("core", mine), beside, send("core", beside)]
+    lines = [mine, send("core", mine), beside, distant, send("core", beside), send("core", distant)]
+    natural, order = list(range(depth)), near + far
     new_references = pl.pallas_call(
-        renew_kernel,
+        functools.partial(renew_kernel, (natural, natural, order, order)),
         out_shape=jax.ShapeDtypeStruct((share, n_own_ref), jnp.float32),
         in_specs=[SMEM] + [VMEM] * (3 + len(lines)),
         out_specs=VMEM,

time: 146 us -> 145 us (level)
  starting transfers between devices: 67.4 us -> 56.7 us
  waiting for transfers between devices: 45.4 us -> 53.3 us
  local copies, waits for them, and re-layouts: 6.25 us -> 12.3 us
  other arithmetic: 3.37 us -> 1.33 us
  Pallas kernels: 22 us -> 20.3 us
    all_to_all x1, waiting for transfers between devices: 0.9 us -> 10.3 us  [local(): parts = lax.all_to_all(parts, 'dom', 0, 0, tiled=True)]
    ppermute x22 -> x20, starting transfers between devices: 42.6 us -> 35.3 us  [send(): return lax.ppermute(value, axis, pairs)]
    ppermute x22 -> x20, waiting for transfers between devices: 23.2 us -> 19.1 us  [send(): return lax.ppermute(value, axis, pairs)]
    unnamed x11 -> x21, local copies, waits for them, and re-layouts: 4.58 us -> 8.5 us
    all_to_all x1, starting transfers between devices: 7.32 us -> 5 us  [local(): lax.all_to_all(weights, ('dom', 'ref'), 0, 0, tiled=True, axis_index_grou...]
    slice x2 -> x1, local copies, waits for them, and re-layouts: 0.02 us -> 2.14 us  [local(): distant = lax.slice_in_dim(mine, lowest, lowest + own_rows)]
    pallas_call x1, Pallas kernels: 4.35 us -> 2.65 us  [local(): pl.pallas_call(functools.partial(score_kernel, counts), out_shape=(jax.Sh...]
    all_to_all x1, waiting for transfers between devices: 14 us -> 15.5 us  [local(): lax.all_to_all(weights, ('dom', 'ref'), 0, 0, tiled=True, axis_index_grou...]
  transfers between devices with their start and end apart: 26 -> 24, of which waited for: 10 -> 9; matrix products, arithmetic and copies ran while one was open for 4% -> 4% of each run, Pallas kernels for 8% -> 7%
where the time goes in v4:
time: 145 us
  starting transfers between devices  56.7 us (39%)
  waiting for transfers between devices  53.3 us (37%)
  Pallas kernels  20.3 us (14%)
  local copies, waits for them, and re-layouts  12.3 us (8%)
    ppermute x20, starting transfers between devices, send(): return lax.ppermute(value, axis, pairs)  35.3 us
    ppermute x20, waiting for transfers between devices, send(): return lax.ppermute(value, axis, pairs)  19.1 us
    all_to_all x1, waiting for transfers between devices, local(): lax.all_to_all(weights, ('dom', 'ref'), 0, 0, tiled=True, axis_index_grou...  15.5 us
    all_to_all x1, waiting for transfers between devices, local(): parts = lax.all_to_all(parts, 'dom', 0, 0, tiled=True)  10.3 us
    unnamed x21, local copies, waits for them, and re-layouts  8.5 us
    all_to_all x1, starting transfers between devices, local(): block = lax.all_to_all(pieces, 'dom', 0, 0, tiled=True)  7.49 us
    pallas_call x1, Pallas kernels, local(): pl.pallas_call(functools.partial(renew_kernel, (natural, natural, order,...  7.24 us
    all_to_all x1, waiting for transfers between devices, local(): lax.all_to_all(stats, 'ref', 0, 0, tiled=True, axis_index_groups=tables['...  5.13 us
  transfers between devices with their start and end apart: 24, of which 9 were waited for; matrix products, arithmetic and copies ran while one was open for 4% of the time, Pallas kernels for 7%

profile of v4, /device:TPU:1, one launch (start us, length us, event | category | flops | bytes accessed | tf_op | source)
XLA Modules:
  0.0 144.7 jit_solution(15503842129676863051)
XLA Ops:
  0.6 3.3 %shard_map.86 = bf16[8,8,2176]{2,1,0:T(8,128)(2,1)} custom-call(s32[2,8]{1,0:T(2,128)} %bitcast.18, s32[8]{0:T(128)} %groups.1, f32[8]{0:T(128)} %precision.1, bf16[8,16384]{1,0:T(8,128)(2,1)} %particles.1, f32[32,16384]{1,0:T(8,128)} %ctf.3), custom_call_target="tpu_custom_call" | custom-call | tf_op jit(solution)/shard_map/pallas_call | solution.py:77
  3.9 7.5 %all-to-all-start = ((bf16[8,8,2176]{2,1,0:T(8,128)(2,1)}), bf16[8,8,2176]{2,1,0:T(8,128)(2,1)S(1)}, u32[]{:S(2)}, u32[]{:S(2)}) async-start(bf16[8,8,2176]{2,1,0:T(8,128)(2,1)} %shard_map.86), calls=%async_computation | async-start | bytes 557056 | tf_op jit(solution)/shard_map/all_to_all | solution.py:299
  11.4 0.6 pad_add_fusion.place
  12.0 3.9 %shard_map.87.refs_9_ = bf16[256,2176]{1,0:T(8,128)(2,1)} custom-call(s32[3]{0:T(128)} %pad_add_fusion.place, bf16[256,16384]{1,0:T(8,128)(2,1)} %references.1, f32[32,16384]{1,0:T(8,128)} %ctf.3), custom_call_target="tpu_custom_call" | custom-call | flops 536870912 | bytes 8388608 | tf_op jit(solution)/shard_map/pallas_call | solution.py:126
  15.9 3.3 %all-to-all-done = bf16[8,8,2176]{2,1,0:T(8,128)(2,1)S(1)} async-done(((bf16[8,8,2176]{2,1,0:T(8,128)(2,1)}), bf16[8,8,2176]{2,1,0:T(8,128)(2,1)S(1)}, u32[]{:S(2)}, u32[]{:S(2)}) %all-to-all-start) | async-done | bytes 278560 | tf_op jit(solution)/shard_map/all_to_all | solution.py:299
  19.1 0.3 collective-permute-start.9
  19.4 1.6 %collective-permute-start.3 = (bf16[64,2176]{1,0:T(8,128)(2,1)S(1)}, bf16[64,2176]{1,0:T(8,128)(2,1)S(1)}, u32[]{:S(2)}, u32[]{:S(2)}) collective-permute-start(bf16[64,2176]{1,0:T(8,128)(2,1)S(1)} %bitcast.12), channel_id=1, source_target_pairs={{0,2},{1,3},{2,4},{3,5},{4,6},{5,7},{6,8},{7,9},{8,10},{9,11},{10,... | collective-permute-start | bytes 835592 | tf_op jit(solution)/shard_map/ppermute | solution.py:275
  21.1 3.9 %collective-permute-start = (bf16[64,2176]{1,0:T(8,128)(2,1)S(1)}, bf16[64,2176]{1,0:T(8,128)(2,1)S(1)}, u32[]{:S(2)}, u32[]{:S(2)}) collective-permute-start(bf16[64,2176]{1,0:T(8,128)(2,1)S(1)} %bitcast.13), channel_id=1, source_target_pairs={{0,14},{1,15},{2,0},{3,1},{4,2},{5,3},{6,4},{7,5},{8,6},{9,7},{10,... | collective-permute-start | bytes 835592 | tf_op jit(solution)/shard_map/ppermute | solution.py:275
  25.0 4.5 %collective-permute-done.3.refs_8_ = bf16[64,2176]{1,0:T(8,128)(2,1)S(1)} collective-permute-done((bf16[64,2176]{1,0:T(8,128)(2,1)S(1)}, bf16[64,2176]{1,0:T(8,128)(2,1)S(1)}, u32[]{:S(2)}, u32[]{:S(2)}) %collective-permute-start.3) | collective-permute-done | bytes 278560 | tf_op jit(solution)/shard_map/ppermute | solution.py:275
  29.5 0.0 collective-permute-start.4
  29.6 0.0 collective-permute-done.refs_1_
  29.6 2.7 %collective-permute-start.1 = (bf16[64,2176]{1,0:T(8,128)(2,1)S(1)}, bf16[64,2176]{1,0:T(8,128)(2,1)S(1)}, u32[]{:S(2)}, u32[]{:S(2)}) collective-permute-start(bf16[64,2176]{1,0:T(8,128)(2,1)S(1)} %collective-permute-done.refs_1_), channel_id=1, source_target_pairs={{0,14},{1,15},{2,0},{3,1},{4,2},{5,3},{6,4},{7,5},{8,6},{9,7},{10,... | collective-permute-start | bytes 835592 | tf_op jit(solution)/shard_map/ppermute | solution.py:275
  32.2 3.9 %collective-permute-done.4.refs_7_ = bf16[64,2176]{1,0:T(8,128)(2,1)S(1)} collective-permute-done((bf16[64,2176]{1,0:T(8,128)(2,1)S(1)}, bf16[64,2176]{1,0:T(8,128)(2,1)S(1)}, u32[]{:S(2)}, u32[]{:S(2)}) %collective-permute-start.4) | collective-permute-done | bytes 278560 | tf_op jit(solution)/shard_map/ppermute | solution.py:275
  36.2 0.0 collective-permute-start.5
  36.2 0.0 collective-permute-done.1.refs_2_
  36.2 2.7 %collective-permute-start.2 = (bf16[64,2176]{1,0:T(8,128)(2,1)S(1)}, bf16[64,2176]{1,0:T(8,128)(2,1)S(1)}, u32[]{:S(2)}, u32[]{:S(2)}) collective-permute-start(bf16[64,2176]{1,0:T(8,128)(2,1)S(1)} %collective-permute-done.1.refs_2_), channel_id=1, source_target_pairs={{0,14},{1,15},{2,0},{3,1},{4,2},{5,3},{6,4},{7,5},{8,6},{9,7},{10,... | collective-permute-start | bytes 835592 | tf_op jit(solution)/shard_map/ppermute | solution.py:275
  38.8 4.9 %collective-permute-start.8 = (bf16[256,2176]{1,0:T(8,128)(2,1)}, bf16[256,2176]{1,0:T(8,128)(2,1)S(1)}, u32[]{:S(2)}, u32[]{:S(2)}) collective-permute-start(bf16[256,2176]{1,0:T(8,128)(2,1)} %shard_map.87.refs_9_), channel_id=1, source_target_pairs={{0,1},{1,0},{2,3},{3,2},{4,5},{5,4},{6,7},{7,6},{8,9},{9,8},{10,11... | collective-permute-start | bytes 3342344 | tf_op jit(solution)/shard_map/ppermute | solution.py:275
  43.8 0.0 collective-permute-done.5.refs_6_
  43.8 4.4 %collective-permute-start.10 = (bf16[256,2176]{1,0:T(8,128)(2,1)S(1)}, bf16[256,2176]{1,0:T(8,128)(2,1)S(1)}, u32[]{:S(2)}, u32[]{:S(2)}) collective-permute-start(bf16[256,2176]{1,0:T(8,128)(2,1)S(1)} %collective-permute-done.9.refs_11_), channel_id=1, source_target_pairs={{0,1},{1,0},{2,3},{3,2},{4,5},{5,4},{6,7},{7,6},{8,9},{9,8},{10,11... | collective-permute-start | bytes 3342344 | tf_op jit(solution)/shard_map/ppermute | solution.py:275
  48.2 1.2 collective-permute-start.11
  49.3 0.1 collective-permute-start.6
  49.5 3.1 %collective-permute-start.7 = (bf16[32,2176]{1,0:T(8,128)(2,1)S(1)}, bf16[32,2176]{1,0:T(8,128)(2,1)S(1)}, u32[]{:S(2)}, u32[]{:S(2)}) collective-permute-start(bf16[32,2176]{1,0:T(8,128)(2,1)S(1)} %slice.13), channel_id=1, source_target_pairs={{0,14},{1,15},{2,0},{3,1},{4,2},{5,3},{6,4},{7,5},{8,6},{9,7},{10,... | collective-permute-start | bytes 417800 | tf_op jit(solution)/shard_map/ppermute | solution.py:275
  52.6 0.0 collective-permute-done.8.refs_10_
  52.6 3.7 %collective-permute-done.6.refs_4_ = bf16[32,2176]{1,0:T(8,128)(2,1)S(1)} collective-permute-done((bf16[32,2176]{1,0:T(8,128)(2,1)S(1)}, bf16[32,2176]{1,0:T(8,128)(2,1)S(1)}, u32[]{:S(2)}, u32[]{:S(2)}) %collective-permute-start.6) | collective-permute-done | bytes 139296 | tf_op jit(solution)/shard_map/ppermute | solution.py:275
  56.3 0.0 collective-permute-done.10.refs_12_
  56.3 1.2 copy-done
  57.6 2.6 %shard_map.88 = (f32[8,64,1024]{2,1,0:T(8,128)S(1)}, bf16[512,2176]{1,0:T(8,128)(2,1)S(1)}) custom-call(bf16[64,2176]{1,0:T(8,128)(2,1)S(1)} %bitcast.15, bf16[64,2176]{1,0:T(8,128)(2,1)S(1)} %collective-permute-done.refs_1_, bf16[64,2176]{1,0:T(8,128)(2,1)S(1)} %collective-permute-done.1.refs_2_, bf16[64,2176]{1,0:T(8,128)(2,1)S(1)} %collective-permute-done.2.refs_3_, ...), custom_call_target="tpu_custom_call" | custom-call | tf_op jit(solution)/shard_map/pallas_call | solution.py:316
  60.3 1.4 copy-done.1
  61.6 1.3 copy-done.3
  62.9 0.0 collective-permute-done.11.refs_0_
  62.9 3.9 %all-to-all-start.1 = ((f32[8,64,1024]{2,1,0:T(8,128)}), f32[8,64,1024]{2,1,0:T(8,128)S(1)}, u32[]{:S(2)}, u32[]{:S(2)}) async-start(f32[8,64,1024]{2,1,0:T(8,128)} %copy-done.3), calls=%async_computation.1 | async-start | bytes 4194304 | tf_op jit(solution)/shard_map/all_to_all | solution.py:327
  66.8 2.2 %collective-permute-start.14 = (bf16[64,2176]{1,0:T(8,128)(2,1)S(1)}, bf16[64,2176]{1,0:T(8,128)(2,1)S(1)}, u32[]{:S(2)}, u32[]{:S(2)}) collective-permute-start(bf16[64,2176]{1,0:T(8,128)(2,1)S(1)} %collective-permute-done.11.refs_0_), channel_id=1, source_target_pairs={{0,2},{1,3},{2,4},{3,5},{4,6},{5,7},{6,8},{7,9},{8,10},{9,11},{10,... | collective-permute-start | bytes 835592 | tf_op jit(solution)/shard_map/ppermute | solution.py:275
  69.0 0.6 collective-permute-start.12
  69.6 1.5 %collective-permute-start.16 = (bf16[512,2176]{1,0:T(8,128)(2,1)}, bf16[512,2176]{1,0:T(8,128)(2,1)}, u32[]{:S(2)}, u32[]{:S(2)}) collective-permute-start(bf16[512,2176]{1,0:T(8,128)(2,1)} %copy-done.1), channel_id=1, source_target_pairs={{0,1},{1,0},{2,3},{3,2},{4,5},{5,4},{6,7},{7,6},{8,9},{9,8},{10,11... | collective-permute-start | bytes 6684680 | tf_op jit(solution)/shard_map/ppermute | solution.py:275
  71.1 4.2 %collective-permute-done.14.refs_4_ = bf16[64,2176]{1,0:T(8,128)(2,1)S(1)} collective-permute-done((bf16[64,2176]{1,0:T(8,128)(2,1)S(1)}, bf16[64,2176]{1,0:T(8,128)(2,1)S(1)}, u32[]{:S(2)}, u32[]{:S(2)}) %collective-permute-start.14) | collective-permute-done | bytes 278560 | tf_op jit(solution)/shard_map/ppermute | solution.py:275
  75.4 0.7 collective-permute-start.15
  76.1 0.0 collective-permute-done.12.refs_1_
  76.1 1.9 %collective-permute-start.13 = (bf16[64,2176]{1,0:T(8,128)(2,1)S(1)}, bf16[64,2176]{1,0:T(8,128)(2,1)S(1)}, u32[]{:S(2)}, u32[]{:S(2)}) collective-permute-start(bf16[64,2176]{1,0:T(8,128)(2,1)S(1)} %collective-permute-done.12.refs_1_), channel_id=1, source_target_pairs={{0,14},{1,15},{2,0},{3,1},{4,2},{5,3},{6,4},{7,5},{8,6},{9,7},{10,... | collective-permute-start | bytes 835592 | tf_op jit(solution)/shard_map/ppermute | solution.py:275
  78.0 2.1 %slice.11 = bf16[192,2176]{1,0:T(8,128)(2,1)} slice(bf16[512,2176]{1,0:T(8,128)(2,1)} %copy-done.1), slice={[192:384], [0:2176]} | slice | bytes 1671168 | tf_op jit(solution)/shard_map/slice | solution.py:359
  80.2 2.7 %collective-permute-done.15.refs_3_ = bf16[64,2176]{1,0:T(8,128)(2,1)S(1)} collective-permute-done((bf16[64,2176]{1,0:T(8,128)(2,1)S(1)}, bf16[64,2176]{1,0:T(8,128)(2,1)S(1)}, u32[]{:S(2)}, u32[]{:S(2)}) %collective-permute-start.15) | collective-permute-done | bytes 278560 | tf_op jit(solution)/shard_map/ppermute | solution.py:275
  82.8 1.0 copy-done.5
  83.8 0.1 shard_map.89.refs_2_
  83.9 10.3 %all-to-all-done.1.parts = f32[8,64,1024]{2,1,0:T(8,128)S(1)} async-done(((f32[8,64,1024]{2,1,0:T(8,128)}), f32[8,64,1024]{2,1,0:T(8,128)S(1)}, u32[]{:S(2)}, u32[]{:S(2)}) %all-to-all-start.1) | async-done | bytes 2097184 | tf_op jit(solution)/shard_map/all_to_all | solution.py:327
  94.2 1.4 shard_map.90
  95.6 0.7 copy-done.6
  96.3 0.9 collective-permute-start.17
  97.3 2.0 %collective-permute-start.18 = (bf16[320,2176]{1,0:T(8,128)(2,1)S(1)}, bf16[320,2176]{1,0:T(8,128)(2,1)}, u32[]{:S(2)}, u32[]{:S(2)}) collective-permute-start(bf16[320,2176]{1,0:T(8,128)(2,1)S(1)} %shard_map.89.refs_2_), channel_id=1, source_target_pairs={{0,1},{1,0},{2,3},{3,2},{4,5},{5,4},{6,7},{7,6},{8,9},{9,8},{10,11... | collective-permute-start | bytes 4177928 | tf_op jit(solution)/shard_map/ppermute | solution.py:275
  99.3 5.0 %all-to-all-start.2 = ((f32[8,1,128]{2,1,0:T(1,128)}), f32[8,1,128]{2,1,0:T(1,128)S(1)}, u32[]{:S(2)}, u32[]{:S(2)}) async-start(f32[8,1,128]{2,1,0:T(1,128)} %get-tuple-element.27), calls=%async_computation.2 | async-start | bytes 8192 | tf_op jit(solution)/shard_map/all_to_all | solution.py:362
  104.3 1.0 constant_dynamic-slice_fusion
  105.3 0.3 copy.13
  105.6 0.1 pad.3.clone
  105.7 5.1 %all-to-all-done.2 = f32[8,1,128]{2,1,0:T(1,128)S(1)} async-done(((f32[8,1,128]{2,1,0:T(1,128)}), f32[8,1,128]{2,1,0:T(1,128)S(1)}, u32[]{:S(2)}, u32[]{:S(2)}) %all-to-all-start.2) | async-done | bytes 4128 | tf_op jit(solution)/shard_map/all_to_all | solution.py:362
  110.8 0.9 copy-done.7
  111.8 1.8 %shard_map.91 = (bf16[32,64,256]{2,1,0:T(8,128)(2,1)}, f32[1,128]{1,0:T(1,128)S(1)}) custom-call(s32[3]{0:T(128)S(1)} %copy-done.8, f32[64,1024]{1,0:T(8,128)S(1)} %copy-done.7, f32[8,128]{1,0:T(8,128)S(1)} %bitcast.16), custom_call_target="tpu_custom_call" | custom-call | tf_op jit(solution)/shard_map/pallas_call | solution.py:363
  113.5 5.0 %all-to-all-start.3 = ((bf16[32,64,256]{2,1,0:T(8,128)(2,1)}), bf16[32,64,256]{2,1,0:T(8,128)(2,1)S(1)}, u32[]{:S(2)}, u32[]{:S(2)}) async-start(bf16[32,64,256]{2,1,0:T(8,128)(2,1)} %get-tuple-element.28), calls=%async_computation.3 | async-start | bytes 2097152 | tf_op jit(solution)/shard_map/all_to_all | solution.py:374
  118.6 0.0 copy-start.9
  118.6 0.4 collective-permute-start.19
  119.0 0.2 fusion
  119.2 0.5 maximum_maximum_fusion.square
  119.7 0.6 dynamic-slice_bitcast_fusion
  120.3 0.0 collective-permute-done.16.refs_1_
  120.3 15.5 %all-to-all-done.3.spread = bf16[32,64,256]{2,1,0:T(8,128)(2,1)S(1)} async-done(((bf16[32,64,256]{2,1,0:T(8,128)(2,1)}), bf16[32,64,256]{2,1,0:T(8,128)(2,1)S(1)}, u32[]{:S(2)}, u32[]{:S(2)}) %all-to-all-start.3) | async-done | bytes 1048608 | tf_op jit(solution)/shard_map/all_to_all | solution.py:374
  135.9 1.6 %copy-done.2 = bf16[512,2176]{1,0:T(8,128)(2,1)S(1)} copy-done((bf16[512,2176]{1,0:T(8,128)(2,1)S(1)}, bf16[512,2176]{1,0:T(8,128)(2,1)}, u32[]{:S(2)}) %copy-start.2) | copy-done | bytes 2228248
  137.5 7.2 %shard_map.92 = f32[2048,256]{1,0:T(8,128)} custom-call(s32[3]{0:T(128)S(1)} %copy-done.8, bf16[32,64,256]{2,1,0:T(8,128)(2,1)S(1)} %all-to-all-done.3.spread, bf16[2048,128]{1,0:T(8,128)(2,1)S(1)} %maximum_maximum_fusion.square, f32[1,256]{1,0:T(1,128)S(1)} %bitcast.17, bf16[512,2176]{1,0:T(8,128)(2,1)S(1)} %copy-done.2, ...), custom_call_target="tpu_custom_call" | custom-call | tf_op jit(solution)/shard_map/pallas_call | solution.py:379
  (22 shorter events, 0.1 us)
Async XLA Ops:
  3.9 15.2 %all-to-all-start = ((bf16[8,8,2176]{2,1,0:T(8,128)(2,1)}), bf16[8,8,2176]{2,1,0:T(8,128)(2,1)S(1)}, u32[]{:S(2)}, u32[]{:S(2)}) async-start(bf16[8,8,2176]{2,1,0:T(8,128)(2,1)} %shard_map.86), calls=%async_computation | async-start | bytes 557056 | tf_op jit(solution)/shard_map/all_to_all | solution.py:299
  19.1 24.6 %collective-permute-start.9 = (bf16[256,2176]{1,0:T(8,128)(2,1)}, bf16[256,2176]{1,0:T(8,128)(2,1)S(1)}, u32[]{:S(2)}, u32[]{:S(2)}) collective-permute-start(bf16[256,2176]{1,0:T(8,128)(2,1)} %shard_map.87.refs_9_), channel_id=1, source_target_pairs={{0,16},{1,17},{2,18},{3,19},{4,20},{5,21},{6,22},{7,23},{8,24},{9,... | collective-permute-start | bytes 3342344 | tf_op jit(solution)/shard_map/ppermute | solution.py:275
  19.4 10.1 %collective-permute-start.3 = (bf16[64,2176]{1,0:T(8,128)(2,1)S(1)}, bf16[64,2176]{1,0:T(8,128)(2,1)S(1)}, u32[]{:S(2)}, u32[]{:S(2)}) collective-permute-start(bf16[64,2176]{1,0:T(8,128)(2,1)S(1)} %bitcast.12), channel_id=1, source_target_pairs={{0,2},{1,3},{2,4},{3,5},{4,6},{5,7},{6,8},{7,9},{8,10},{9,11},{10,... | collective-permute-start | bytes 835592 | tf_op jit(solution)/shard_map/ppermute | solution.py:275
  21.1 8.5 %collective-permute-start = (bf16[64,2176]{1,0:T(8,128)(2,1)S(1)}, bf16[64,2176]{1,0:T(8,128)(2,1)S(1)}, u32[]{:S(2)}, u32[]{:S(2)}) collective-permute-start(bf16[64,2176]{1,0:T(8,128)(2,1)S(1)} %bitcast.13), channel_id=1, source_target_pairs={{0,14},{1,15},{2,0},{3,1},{4,2},{5,3},{6,4},{7,5},{8,6},{9,7},{10,... | collective-permute-start | bytes 835592 | tf_op jit(solution)/shard_map/ppermute | solution.py:275
  29.5 6.6 %collective-permute-start.4 = (bf16[64,2176]{1,0:T(8,128)(2,1)S(1)}, bf16[64,2176]{1,0:T(8,128)(2,1)S(1)}, u32[]{:S(2)}, u32[]{:S(2)}) collective-permute-start(bf16[64,2176]{1,0:T(8,128)(2,1)S(1)} %collective-permute-done.3.refs_8_), channel_id=1, source_target_pairs={{0,2},{1,3},{2,4},{3,5},{4,6},{5,7},{6,8},{7,9},{8,10},{9,11},{10,... | collective-permute-start | bytes 835592 | tf_op jit(solution)/shard_map/ppermute | solution.py:275
  29.6 6.6 %collective-permute-start.1 = (bf16[64,2176]{1,0:T(8,128)(2,1)S(1)}, bf16[64,2176]{1,0:T(8,128)(2,1)S(1)}, u32[]{:S(2)}, u32[]{:S(2)}) collective-permute-start(bf16[64,2176]{1,0:T(8,128)(2,1)S(1)} %collective-permute-done.refs_1_), channel_id=1, source_target_pairs={{0,14},{1,15},{2,0},{3,1},{4,2},{5,3},{6,4},{7,5},{8,6},{9,7},{10,... | collective-permute-start | bytes 835592 | tf_op jit(solution)/shard_map/ppermute | solution.py:275
  36.2 7.6 %collective-permute-start.5 = (bf16[64,2176]{1,0:T(8,128)(2,1)S(1)}, bf16[64,2176]{1,0:T(8,128)(2,1)S(1)}, u32[]{:S(2)}, u32[]{:S(2)}) collective-permute-start(bf16[64,2176]{1,0:T(8,128)(2,1)S(1)} %collective-permute-done.4.refs_7_), channel_id=1, source_target_pairs={{0,2},{1,3},{2,4},{3,5},{4,6},{5,7},{6,8},{7,9},{8,10},{9,11},{10,... | collective-permute-start | bytes 835592 | tf_op jit(solution)/shard_map/ppermute | solution.py:275
  36.2 7.6 %collective-permute-start.2 = (bf16[64,2176]{1,0:T(8,128)(2,1)S(1)}, bf16[64,2176]{1,0:T(8,128)(2,1)S(1)}, u32[]{:S(2)}, u32[]{:S(2)}) collective-permute-start(bf16[64,2176]{1,0:T(8,128)(2,1)S(1)} %collective-permute-done.1.refs_2_), channel_id=1, source_target_pairs={{0,14},{1,15},{2,0},{3,1},{4,2},{5,3},{6,4},{7,5},{8,6},{9,7},{10,... | collective-permute-start | bytes 835592 | tf_op jit(solution)/shard_map/ppermute | solution.py:275
  38.8 13.8 %collective-permute-start.8 = (bf16[256,2176]{1,0:T(8,128)(2,1)}, bf16[256,2176]{1,0:T(8,128)(2,1)S(1)}, u32[]{:S(2)}, u32[]{:S(2)}) collective-permute-start(bf16[256,2176]{1,0:T(8,128)(2,1)} %shard_map.87.refs_9_), channel_id=1, source_target_pairs={{0,1},{1,0},{2,3},{3,2},{4,5},{5,4},{6,7},{7,6},{8,9},{9,8},{10,11... | collective-permute-start | bytes 3342344 | tf_op jit(solution)/shard_map/ppermute | solution.py:275
  43.8 12.6 %collective-permute-start.10 = (bf16[256,2176]{1,0:T(8,128)(2,1)S(1)}, bf16[256,2176]{1,0:T(8,128)(2,1)S(1)}, u32[]{:S(2)}, u32[]{:S(2)}) collective-permute-start(bf16[256,2176]{1,0:T(8,128)(2,1)S(1)} %collective-permute-done.9.refs_11_), channel_id=1, source_target_pairs={{0,1},{1,0},{2,3},{3,2},{4,5},{5,4},{6,7},{7,6},{8,9},{9,8},{10,11... | collective-permute-start | bytes 3342344 | tf_op jit(solution)/shard_map/ppermute | solution.py:275
  48.2 14.8 %collective-permute-start.11 = (bf16[64,2176]{1,0:T(8,128)(2,1)S(1)}, bf16[64,2176]{1,0:T(8,128)(2,1)S(1)}, u32[]{:S(2)}, u32[]{:S(2)}) collective-permute-start(bf16[64,2176]{1,0:T(8,128)(2,1)S(1)} %bitcast.14), channel_id=1, source_target_pairs={{0,16},{1,17},{2,18},{3,19},{4,20},{5,21},{6,22},{7,23},{8,24},{9,... | collective-permute-start | bytes 835592 | tf_op jit(solution)/shard_map/ppermute | solution.py:275
  49.3 7.0 %collective-permute-start.6 = (bf16[32,2176]{1,0:T(8,128)(2,1)S(1)}, bf16[32,2176]{1,0:T(8,128)(2,1)S(1)}, u32[]{:S(2)}, u32[]{:S(2)}) collective-permute-start(bf16[32,2176]{1,0:T(8,128)(2,1)S(1)} %slice.12), channel_id=1, source_target_pairs={{0,2},{1,3},{2,4},{3,5},{4,6},{5,7},{6,8},{7,9},{8,10},{9,11},{10,... | collective-permute-start | bytes 417800 | tf_op jit(solution)/shard_map/ppermute | solution.py:275
  49.5 6.9 %collective-permute-start.7 = (bf16[32,2176]{1,0:T(8,128)(2,1)S(1)}, bf16[32,2176]{1,0:T(8,128)(2,1)S(1)}, u32[]{:S(2)}, u32[]{:S(2)}) collective-permute-start(bf16[32,2176]{1,0:T(8,128)(2,1)S(1)} %slice.13), channel_id=1, source_target_pairs={{0,14},{1,15},{2,0},{3,1},{4,2},{5,3},{6,4},{7,5},{8,6},{9,7},{10,... | collective-permute-start | bytes 417800 | tf_op jit(solution)/shard_map/ppermute | solution.py:275
  56.3 1.2 copy-start
  60.2 1.4 copy-start.1
  61.6 1.3 copy-start.3
  62.9 6.1 %copy-start.4 = (bf16[64,2176]{1,0:T(8,128)(2,1)}, bf16[64,2176]{1,0:T(8,128)(2,1)S(1)}, u32[]{:S(2)}) copy-start(bf16[64,2176]{1,0:T(8,128)(2,1)S(1)} %collective-permute-done.11.refs_0_) | copy-start | bytes 835588
  62.9 31.3 %all-to-all-start.1 = ((f32[8,64,1024]{2,1,0:T(8,128)}), f32[8,64,1024]{2,1,0:T(8,128)S(1)}, u32[]{:S(2)}, u32[]{:S(2)}) async-start(f32[8,64,1024]{2,1,0:T(8,128)} %copy-done.3), calls=%async_computation.1 | async-start | bytes 4194304 | tf_op jit(solution)/shard_map/all_to_all | solution.py:327
  66.8 8.5 %collective-permute-start.14 = (bf16[64,2176]{1,0:T(8,128)(2,1)S(1)}, bf16[64,2176]{1,0:T(8,128)(2,1)S(1)}, u32[]{:S(2)}, u32[]{:S(2)}) collective-permute-start(bf16[64,2176]{1,0:T(8,128)(2,1)S(1)} %collective-permute-done.11.refs_0_), channel_id=1, source_target_pairs={{0,2},{1,3},{2,4},{3,5},{4,6},{5,7},{6,8},{7,9},{8,10},{9,11},{10,... | collective-permute-start | bytes 835592 | tf_op jit(solution)/shard_map/ppermute | solution.py:275
  69.0 7.0 %collective-permute-start.12 = (bf16[64,2176]{1,0:T(8,128)(2,1)S(1)}, bf16[64,2176]{1,0:T(8,128)(2,1)S(1)}, u32[]{:S(2)}, u32[]{:S(2)}) collective-permute-start(bf16[64,2176]{1,0:T(8,128)(2,1)S(1)} %collective-permute-done.11.refs_0_), channel_id=1, source_target_pairs={{0,14},{1,15},{2,0},{3,1},{4,2},{5,3},{6,4},{7,5},{8,6},{9,7},{10,... | collective-permute-start | bytes 835592 | tf_op jit(solution)/shard_map/ppermute | solution.py:275
  69.6 24.6 %copy-start.8 = (s32[3]{0:T(128)S(1)}, s32[3]{0:T(128)}, u32[]{:S(2)}) copy-start(s32[3]{0:T(128)} %pad_add_fusion.place) | copy-start | bytes 40
  69.6 50.7 %collective-permute-start.16 = (bf16[512,2176]{1,0:T(8,128)(2,1)}, bf16[512,2176]{1,0:T(8,128)(2,1)}, u32[]{:S(2)}, u32[]{:S(2)}) collective-permute-start(bf16[512,2176]{1,0:T(8,128)(2,1)} %copy-done.1), channel_id=1, source_target_pairs={{0,1},{1,0},{2,3},{3,2},{4,5},{5,4},{6,7},{7,6},{8,9},{9,8},{10,11... | collective-permute-start | bytes 6684680 | tf_op jit(solution)/shard_map/ppermute | solution.py:275
  75.4 7.5 %collective-permute-start.15 = (bf16[64,2176]{1,0:T(8,128)(2,1)S(1)}, bf16[64,2176]{1,0:T(8,128)(2,1)S(1)}, u32[]{:S(2)}, u32[]{:S(2)}) collective-permute-start(bf16[64,2176]{1,0:T(8,128)(2,1)S(1)} %collective-permute-done.14.refs_4_), channel_id=1, source_target_pairs={{0,2},{1,3},{2,4},{3,5},{4,6},{5,7},{6,8},{7,9},{8,10},{9,11},{10,... | collective-permute-start | bytes 835592 | tf_op jit(solution)/shard_map/ppermute | solution.py:275
  76.1 6.8 %collective-permute-start.13 = (bf16[64,2176]{1,0:T(8,128)(2,1)S(1)}, bf16[64,2176]{1,0:T(8,128)(2,1)S(1)}, u32[]{:S(2)}, u32[]{:S(2)}) collective-permute-start(bf16[64,2176]{1,0:T(8,128)(2,1)S(1)} %collective-permute-done.12.refs_1_), channel_id=1, source_target_pairs={{0,14},{1,15},{2,0},{3,1},{4,2},{5,3},{6,4},{7,5},{8,6},{9,7},{10,... | collective-permute-start | bytes 835592 | tf_op jit(solution)/shard_map/ppermute | solution.py:275
  82.8 1.0 copy-start.5
  95.6 0.7 copy-start.6
  96.3 22.2 %collective-permute-start.17 = (bf16[192,2176]{1,0:T(8,128)(2,1)}, bf16[192,2176]{1,0:T(8,128)(2,1)}, u32[]{:S(2)}, u32[]{:S(2)}) collective-permute-start(bf16[192,2176]{1,0:T(8,128)(2,1)} %slice.11), channel_id=1, source_target_pairs={{0,16},{1,17},{2,18},{3,19},{4,20},{5,21},{6,22},{7,23},{8,24},{9,... | collective-permute-start | bytes 2506760 | tf_op jit(solution)/shard_map/ppermute | solution.py:275
  97.3 38.6 %collective-permute-start.18 = (bf16[320,2176]{1,0:T(8,128)(2,1)S(1)}, bf16[320,2176]{1,0:T(8,128)(2,1)}, u32[]{:S(2)}, u32[]{:S(2)}) collective-permute-start(bf16[320,2176]{1,0:T(8,128)(2,1)S(1)} %shard_map.89.refs_2_), channel_id=1, source_target_pairs={{0,1},{1,0},{2,3},{3,2},{4,5},{5,4},{6,7},{7,6},{8,9},{9,8},{10,11... | collective-permute-start | bytes 4177928 | tf_op jit(solution)/shard_map/ppermute | solution.py:275
  99.3 11.5 %all-to-all-start.2 = ((f32[8,1,128]{2,1,0:T(1,128)}), f32[8,1,128]{2,1,0:T(1,128)S(1)}, u32[]{:S(2)}, u32[]{:S(2)}) async-start(f32[8,1,128]{2,1,0:T(1,128)} %get-tuple-element.27), calls=%async_computation.2 | async-start | bytes 8192 | tf_op jit(solution)/shard_map/all_to_all | solution.py:362
  110.8 1.0 copy-start.7
  113.5 22.3 %all-to-all-start.3 = ((bf16[32,64,256]{2,1,0:T(8,128)(2,1)}), bf16[32,64,256]{2,1,0:T(8,128)(2,1)S(1)}, u32[]{:S(2)}, u32[]{:S(2)}) async-start(bf16[32,64,256]{2,1,0:T(8,128)(2,1)} %get-tuple-element.28), calls=%async_computation.3 | async-start | bytes 2097152 | tf_op jit(solution)/shard_map/all_to_all | solution.py:374
  118.6 17.3 %copy-start.9 = (f32[256]{0:T(256)S(1)}, f32[256]{0:T(256)}, u32[]{:S(2)}) copy-start(f32[256]{0:T(256)} %param.13) | copy-start | bytes 3076
  118.6 17.3 %collective-permute-start.19 = (bf16[192,2176]{1,0:T(8,128)(2,1)}, bf16[192,2176]{1,0:T(8,128)(2,1)}, u32[]{:S(2)}, u32[]{:S(2)}) collective-permute-start(bf16[192,2176]{1,0:T(8,128)(2,1)} %collective-permute-done.17.refs_3_), channel_id=1, source_target_pairs={{0,1},{1,0},{2,3},{3,2},{4,5},{5,4},{6,7},{7,6},{8,9},{9,8},{10,11... | collective-permute-start | bytes 2506760 | tf_op jit(solution)/shard_map/ppermute | solution.py:275
  135.8 1.6 %copy-start.2 = (bf16[512,2176]{1,0:T(8,128)(2,1)S(1)}, bf16[512,2176]{1,0:T(8,128)(2,1)}, u32[]{:S(2)}) copy-start(bf16[512,2176]{1,0:T(8,128)(2,1)} %copy-done.1) | copy-start | bytes 6684676
